TPU v7x, 256 devices: a whole 4x4x8 slice. The times are simulated.
256 devices in a mesh: replica: 32 (over y_hi, z, core), tensor: 8 (over x, y_lo).
Axes of the slice: x: 4, y: 4 (y_hi: 2, y_lo: 2; y = y_hi * 2 + y_lo), z: 8, core: 2. Of those that a mesh axis runs over, the one named last changes fastest.
Arguments:
- hidden: bfloat16 [1024, 2, 5120], P('replica'), may hold values from -6 to 6
- queries: bfloat16 [1024, 2, 4096], P('replica', None, 'tensor'), may hold values from -170 to 170
- cache_keys: bfloat16 [1024, 256, 1024], P('replica', None, 'tensor'), may hold values from -6 to 6
- cache_values: bfloat16 [1024, 256, 1024], P('replica', None, 'tensor'), may hold values from -6 to 6
- key_weight: bfloat16 [5120, 1024], P(None, 'tensor'), may hold values from -0.078125 to 0.078125
- value_weight: bfloat16 [5120, 1024], P(None, 'tensor'), may hold values from -0.078125 to 0.078125
- key_gain: float32 [128], replicated, may hold values from 0.1 to 1.9
- out_weight: bfloat16 [4096, 5120], P('tensor'), may hold values from -0.09375 to 0.09375
- lengths: int32 [1024], replicated, may hold values from 0 to 254, as said below
- move_src: int32 [448], replicated, may hold values from 0 to 1023, as said below
- move_dst: int32 [448], replicated, may hold values from 1 to 1022, as said below
Outputs:
- attn_branch: bfloat16 [1024, 2, 5120], P('replica', None, 'tensor')
- keys_out: bfloat16 [1024, 256, 1024], P('replica', None, 'tensor')
- values_out: bfloat16 [1024, 256, 1024], P('replica', None, 'tensor')
Inputs may be any that keep to these rules, and one draw needn't show every extreme that they name: `lengths`: every replica has exactly 14 slots with length 0 and all its other slots hold 2 or more tokens; some slot holds exactly 254. `move_src`: entries k * 14 to (k + 1) * 14 - 1 are slots of replica k; all are distinct slots with nonzero length; slots 0 and 1023 always leave. `move_dst`: all distinct slots of length 0; every replica receives exactly 14 rollouts; no move stays within a replica, and no two moves go from the same replica to the same replica; slots 1 and 1022 always receive.
All inputs are finite; a program needn't handle non-finite values.
Results may differ from a plain program's by a relative error of at most 0.0058.
Values may be sent and summed in bfloat16 or wider, within the bound.
A program may use at most 64 MiB of HBM per device.

v0:
```python
import math

import jax
import jax.numpy as jnp
from jax import lax
from jax.sharding import PartitionSpec as P

EPS = 1e-06
THETA = 1000000.0


def rotate(vectors, positions):
    half_width = vectors.shape[-1] // 2
    indices = jnp.arange(half_width, dtype=jnp.float32)
    frequency = jnp.exp(indices * (-2.0 * math.log(THETA) / vectors.shape[-1]))
    angles = positions[:, :, None, None] * frequency
    cosine = jnp.cos(angles)
    sine_values = jnp.sin(angles)
    former = vectors[..., :half_width]
    latter = vectors[..., half_width:]
    return jnp.concatenate(
        [former * cosine - latter * sine_values, latter * cosine + former * sine_values], -1
    )


def new_entries(hidden, key_weight, value_weight, key_gain, length):
    row_count = hidden.shape[0]
    flat_rows = hidden.reshape(row_count * 2, hidden.shape[2])
    raw_keys = jnp.dot(flat_rows, key_weight, preferred_element_type=jnp.float32).reshape(
        row_count, 2, -1, key_gain.shape[0]
    )
    mean_square = jnp.mean(raw_keys * raw_keys, axis=-1, keepdims=True)
    normed = raw_keys * lax.rsqrt(mean_square + EPS) * key_gain
    positions = (length[:, None] + jnp.arange(2, dtype=jnp.int32)[None, :]).astype(jnp.float32)
    fresh_keys = rotate(normed, positions).reshape(row_count, 2, -1).astype(jnp.bfloat16)
    fresh_values = (
        jnp.dot(flat_rows, value_weight, preferred_element_type=jnp.float32)
        .reshape(row_count, 2, -1)
        .astype(jnp.bfloat16)
    )
    return (fresh_keys, fresh_values)


def place(stored, fresh, length, active):
    row_ids = jnp.arange(stored.shape[1], dtype=jnp.int32)[None, :, None]
    border = length[:, None, None]
    kept = jnp.where(row_ids < border, stored, jnp.zeros_like(stored))
    kept = jnp.where(row_ids == border, fresh[:, 0:1, :], kept)
    kept = jnp.where(row_ids == border + 1, fresh[:, 1:2, :], kept)
    return jnp.where(active[:, None, None], kept, jnp.zeros_like(kept))


def attend(full_keys, full_values, length, queries, head_dim):
    row_count, key_rows, width = full_keys.shape
    kv_heads = width // head_dim
    group_size = queries.shape[-1] // width
    query_heads = queries.reshape(row_count, 2, kv_heads, group_size, head_dim)
    key_heads = full_keys.reshape(row_count, key_rows, kv_heads, head_dim)
    value_heads = full_values.reshape(row_count, key_rows, kv_heads, head_dim)
    scores = jnp.einsum(
        "rsvgh,rlvh->rvsgl", query_heads, key_heads, preferred_element_type=jnp.float32
    ) * head_dim ** (-0.5)
    row_ids = jnp.arange(key_rows, dtype=jnp.int32)[None, None, :]
    limits = length[:, None, None] + jnp.arange(2, dtype=jnp.int32)[None, :, None]
    visible = row_ids <= limits
    scores = jnp.where(visible[:, None, :, None, :], scores, -jnp.inf)
    highest = jnp.max(scores, axis=-1, keepdims=True)
    weights = jnp.exp(scores - highest)
    shares = (weights / jnp.sum(weights, axis=-1, keepdims=True)).astype(jnp.bfloat16)
    mixture = jnp.einsum(
        "rvsgl,rlvh->rsvgh", shares, value_heads, preferred_element_type=jnp.float32
    )
    return mixture.reshape(row_count, 2, -1).astype(jnp.bfloat16)


def shards(
    hidden,
    queries,
    cache_keys,
    cache_values,
    key_weight,
    value_weight,
    key_gain,
    out_weight,
    lengths,
    move_src,
    move_dst,
):
    local_count = cache_keys.shape[0]
    replicas = lax.axis_size("replica")
    replica_here = lax.axis_index("replica")
    first_slot = replica_here * local_count
    head_dim = key_gain.shape[0]
    all_slots = jnp.arange(lengths.shape[0], dtype=jnp.int32)
    anchor = all_slots.at[move_src].set(-1).at[move_dst].set(move_src)
    own_anchor = lax.dynamic_slice_in_dim(anchor, first_slot, local_count)
    holding = own_anchor >= 0
    new_length = jnp.where(holding, lengths[jnp.where(holding, own_anchor, 0)], 0)
    alive = new_length > 0
    local_ids = first_slot + jnp.arange(local_count, dtype=jnp.int32)
    source_rep = move_src // local_count
    target_rep = move_dst // local_count
    peer_ids = jnp.arange(replicas, dtype=jnp.int32)
    sending = (source_rep[None, :] == replica_here) & (target_rep[None, :] == peer_ids[:, None])
    has_out = jnp.any(sending, axis=1)
    send_slot = jnp.sum(jnp.where(sending, move_src[None, :] - first_slot, 0), axis=1)
    outbound = has_out[:, None, None]
    pack_keys = jnp.where(outbound, cache_keys[send_slot], jnp.zeros((), cache_keys.dtype))
    pack_values = jnp.where(outbound, cache_values[send_slot], jnp.zeros((), cache_values.dtype))
    arrived_keys, arrived_values = (
        lax.all_to_all(pack_keys, "replica", split_axis=0, concat_axis=0, tiled=True),
        lax.all_to_all(pack_values, "replica", split_axis=0, concat_axis=0, tiled=True),
    )
    arriving = move_dst[None, :] == local_ids[:, None]
    incoming = jnp.any(arriving, axis=1)
    from_rep = jnp.sum(jnp.where(arriving, source_rep[None, :], 0), axis=1)
    leaving = jnp.any(move_src[None, :] == local_ids[:, None], axis=1)
    inbound = incoming[:, None, None]
    staying = (~leaving)[:, None, None]
    zero_key = jnp.zeros((), cache_keys.dtype)
    kept_keys = jnp.where(staying, cache_keys, zero_key)
    kept_values = jnp.where(staying, cache_values, zero_key)
    base_keys = jnp.where(inbound, arrived_keys[from_rep], kept_keys)
    base_values = jnp.where(inbound, arrived_values[from_rep], kept_values)
    fresh_keys, fresh_values = new_entries(hidden, key_weight, value_weight, key_gain, new_length)
    keys_out = place(base_keys, fresh_keys, new_length, alive)
    values_out = place(base_values, fresh_values, new_length, alive)
    mixture = attend(keys_out, values_out, new_length, queries, head_dim)
    head_terms = jnp.dot(
        mixture.reshape(local_count * 2, -1), out_weight, preferred_element_type=jnp.float32
    )
    head_terms = head_terms.reshape(local_count, 2, -1)
    head_terms = jnp.where(alive[:, None, None], head_terms, 0.0)
    attn_branch = lax.psum_scatter(head_terms, "tensor", scatter_dimension=2, tiled=True).astype(
        jnp.bfloat16
    )
    return (attn_branch, keys_out, values_out)


def solution(mesh):
    placed = (
        P("replica", None, None),
        P("replica", None, "tensor"),
        P("replica", None, "tensor"),
        P("replica", None, "tensor"),
        P(None, "tensor"),
        P(None, "tensor"),
        P(),
        P("tensor", None),
        P(),
        P(),
        P(),
    )
    return jax.shard_map(
        shards,
        mesh=mesh,
        in_specs=placed,
        out_specs=(
            P("replica", None, "tensor"),
            P("replica", None, "tensor"),
            P("replica", None, "tensor"),
        ),
        check_vma=False,
    )
```

profile of v0, /device:TPU:1, one launch (start us, length us, event | category | flops | bytes accessed | tf_op | source)
XLA Modules:
  0.0 204.1 jit_solution(14796583267388762879)
XLA Ops:
  7.2 0.0 copy-start
  7.2 0.8 broadcast_subtract_fusion
  8.0 0.7 broadcast_compare_fusion
  8.7 0.7 add_select_fusion
  9.4 0.1 fusion.33
  9.5 0.9 fusion.30
  10.4 0.0 copy-start.2
  10.4 3.9 %gather_fusion.1 = bf16[32,256,128]{2,1,0:T(8,128)(2,1)} fusion(bf16[32,256,128]{2,1,0:T(8,128)(2,1)} %param.14, s32[1024]{0:T(1024)S(1)} %pad_clamp_fusion.1), kind=kCustom, calls=%fused_computation.1 | custom fusion | bytes 4194432 | tf_op jit(solution)/shard_map/gather | solution.py:109
  14.3 0.0 copy-done.2
  14.3 2.1 %gather_fusion.3 = bf16[32,256,128]{2,1,0:T(8,128)(2,1)} fusion(bf16[32,256,128]{2,1,0:T(8,128)(2,1)S(1)} %copy-done.2, s32[1024]{0:T(1024)S(1)} %pad_clamp_fusion.1), kind=kCustom, calls=%fused_computation.3 | custom fusion | bytes 4194432 | tf_op jit(solution)/shard_map/gather | solution.py:108
  16.4 3.9 %broadcast_select_fusion = (bf16[32,256,128]{2,1,0:T(8,128)(2,1)}, bf16[32,256,128]{2,1,0:T(8,128)(2,1)S(1)}) fusion(bf16[32,256,128]{2,1,0:T(8,128)(2,1)} %gather_fusion.3, pred[32]{0:T(512)(128)(4,1)S(1)} %fusion.33, bf16[32,256,128]{2,1,0:T(8,128)(2,1)} %gather_fusion.1), kind=kLoop, calls=%fused_computation.16 | loop fusion | flops 2097152 | bytes 8388640 | tf_op jit(solution)/shard_map/jit(_where)/select_n | solution.py:108
  20.3 62.9 %all_to_all.10 = bf16[32,256,128]{2,1,0:T(8,128)(2,1)} all-to-all(bf16[32,256,128]{2,1,0:T(8,128)(2,1)S(1)} %get-tuple-element.33), channel_id=1, replica_groups=mesh['replica'=32,'tensor'=8] {'replica'}, dimensions={0} | all-to-all | bytes 4194304 | tf_op jit(solution)/shard_map/all_to_all | solution.py:112
  83.1 6.2 %all-to-all-start.1 = ((bf16[32,256,128]{2,1,0:T(8,128)(2,1)}), bf16[32,256,128]{2,1,0:T(8,128)(2,1)S(1)}, u32[]{:S(2)}, u32[]{:S(2)}) async-start(bf16[32,256,128]{2,1,0:T(8,128)(2,1)} %get-tuple-element.32), calls=%async_computation.1 | async-start | bytes 4194304 | tf_op jit(solution)/shard_map/all_to_all | solution.py:111
  89.4 0.0 copy-start.6
  89.4 0.0 copy-start.7
  89.4 0.0 reduce-scatter.2.cloned.1.call-start
  89.4 2.8 %reshape.286 = bf16[64,5120]{1,0:T(8,128)(2,1)} reshape(bf16[32,2,5120]{2,1,0:T(2,128)(2,1)} %param.11) | data formatting | bytes 1310720 | tf_op jit(solution)/shard_map/reshape | solution.py:28
  92.2 0.0 copy-done
  92.2 1.6 multiply_reduce_fusion
  93.8 0.1 rsqrt.12
  93.9 0.1 copy.25
  94.0 0.0 copy-done.6
  94.0 0.0 copy-done.7
  94.0 0.7 compare_reduce_fusion
  94.7 0.5 not.7
  95.2 2.9 %scatter_fusion = s32[1024]{0:T(1024)S(1)} fusion(s32[1024]{0:T(1024)S(1)} %iota.53, s32[448]{0:T(512)S(1)} %get-tuple-element.29, s32[448]{0:T(512)S(1)} %broadcast.242), kind=kCustom, calls=%fused_computation.5 | custom fusion | bytes 7168 | tf_op jit(solution)/shard_map/scatter | solution.py:95
  98.1 0.0 copy-start.1
  98.1 0.0 copy-start.4
  98.1 0.0 copy-start.9
  98.1 2.9 %scatter_fusion.1 = s32[1024]{0:T(1024)S(1)} fusion(s32[1024]{0:T(1024)S(1)} %scatter_fusion, s32[448]{0:T(512)S(1)} %get-tuple-element.27, s32[448]{0:T(512)S(1)} %copy-done.6), kind=kCustom, calls=%fused_computation.6 | custom fusion | bytes 7168 | tf_op jit(solution)/shard_map/scatter | solution.py:95
  101.1 0.1 compare_select_fusion.3
  101.1 0.0 copy-done.1
  101.1 0.7 gather_fusion
  101.8 0.1 broadcast_add_fusion
  101.9 0.1 copy.24
  102.0 0.0 copy-done.4
  102.0 0.7 reshape.288
  102.7 0.0 copy-done.9
  102.7 0.1 fusion.42
  102.8 0.2 fusion.39
  103.0 0.1 maximum_bitcast_fusion
  103.1 0.5 broadcast_compare_fusion.1
  103.6 0.1 iota_compare_fusion.3
  103.7 0.1 iota_compare_fusion
  103.8 1.9 fusion.25
  105.7 0.6 slice_bitcast_fusion.1
  106.3 3.7 %gather_fusion.2 = bf16[32,256,128]{2,1,0:T(8,128)(2,1)} fusion(bf16[32,256,128]{2,1,0:T(8,128)(2,1)} %all_to_all.10, s32[1024]{0:T(1024)S(1)} %pad_clamp_fusion), kind=kCustom, calls=%fused_computation.2 | custom fusion | bytes 4194432 | tf_op jit(solution)/shard_map/gather | solution.py:124
  110.0 30.2 %all-to-all-done.1 = bf16[32,256,128]{2,1,0:T(8,128)(2,1)S(1)} async-done(((bf16[32,256,128]{2,1,0:T(8,128)(2,1)}), bf16[32,256,128]{2,1,0:T(8,128)(2,1)S(1)}, u32[]{:S(2)}, u32[]{:S(2)}) %all-to-all-start.1) | async-done | bytes 2097184 | tf_op jit(solution)/shard_map/all_to_all | solution.py:111
  140.3 2.1 %gather_fusion.4 = bf16[32,256,128]{2,1,0:T(8,128)(2,1)} fusion(bf16[32,256,128]{2,1,0:T(8,128)(2,1)S(1)} %all-to-all-done.1, s32[1024]{0:T(1024)S(1)} %pad_clamp_fusion), kind=kCustom, calls=%fused_computation.4 | custom fusion | bytes 4194432 | tf_op jit(solution)/shard_map/gather | solution.py:123
  142.4 0.0 copy-start.5
  142.4 7.8 %select_select_fusion = (bf16[32,256,128]{2,1,0:T(8,128)(2,1)S(1)}, bf16[32,256,128]{2,1,0:T(8,128)(2,1)}) fusion(bf16[32,256,128]{2,1,0:T(8,128)(2,1)} %gather_fusion.4, bf16[32,256,128]{2,1,0:T(8,128)(2,1)} %param.13, pred[32]{0:T(512)(128)(4,1)} %not.7, pred[32]{0:T(512)(128)(4,1)} %get-tuple-element.12, pred[32]{0:T(512)(128)(4,1)} %broadcast_compare_fusion.1, ...), kind=kLoop, calls=%fused_computation.14 | loop fusion | flops 12582912 | bytes 12640352 | tf_op jit(solution)/shard_map/jit(_where)/select_n | solution.py:50
  150.2 0.0 copy-start.3
  150.2 0.0 copy-done.5
  150.2 2.1 %fusion.50 = (f32[32,2,4]{2,1,0:T(2,128)}, f32[32,2,4,256]{3,2,1,0:T(4,128)}) fusion(bf16[32,2,4,128]{3,2,1,0:T(4,128)(2,1)S(1)} %copy-done.5, bf16[32,256,128]{2,1,0:T(8,128)(2,1)S(1)} %get-tuple-element.20, pred[32,2,256]{2,1,0:T(4,128)(4,1)S(1)} %iota_compare_fusion), kind=kOutput, calls=%fused_computation.97 | convolution fusion | flops 17039616 | bytes 2442240 | tf_op jit(solution)/shard_map/sub | solution.py:68
  152.3 0.0 copy-start.8
  152.3 2.1 %fusion.22 = bf16[32,2,1,4,128]{4,3,1,0,2:T(4,128)(2,1)S(1)} fusion(bf16[32,256,128]{2,1,0:T(8,128)(2,1)} %get-tuple-element.21, f32[32,2,4,256]{3,2,1,0:T(4,128)} %get-tuple-element.39, f32[32,2,4]{2,1,0:T(2,128)} %get-tuple-element.38), kind=kOutput, calls=%fused_computation.26 | convolution fusion | flops 16941056 | bytes 2425856 | tf_op jit(solution)/shard_map/rvsgl,rlvh->rsvgh/dot_general | solution.py:70
  154.4 0.0 copy-done.3
  154.5 0.0 copy-done.8
  154.5 4.6 %convolution_select_fusion = f32[32,2,5120]{2,0,1:T(8,128)} fusion(bf16[512,5120]{1,0:T(8,128)(2,1)} %param.18, pred[32]{0:T(512)(128)(4,1)S(1)} %copy-done.8, bf16[32,2,512]{2,1,0:T(2,128)(2,1)S(1)} %convert_element_type.42), kind=kOutput, calls=%fused_computation.8 | convolution fusion | flops 335872000 | bytes 6619168 | tf_op jit(solution)/shard_map/dot_general | solution.py:129
  159.0 0.0 reduce-scatter.2.cloned.1.call-update
  159.1 36.5 %reduce-scatter.2.cloned.1.call-done = f32[32,2,640]{2,0,1:T(8,128)} async-done(((f32[32,2,5120]{2,0,1:T(8,128)}), f32[32,2,640]{2,0,1:T(8,128)}) %reduce-scatter.2.cloned.1.call-update) | async-done | bytes 163856 | tf_op jit(solution)/shard_map/reduce_scatter | solution.py:134
  195.6 0.9 convert_element_type.43
  196.5 0.7 copy.28
  (12 shorter events, 0.1 us)
Async XLA Ops:
  7.2 85.0 %copy-start = (bf16[5120,128]{1,0:T(8,128)(2,1)S(1)}, bf16[5120,128]{1,0:T(8,128)(2,1)}, u32[]{:S(2)}) copy-start(bf16[5120,128]{1,0:T(8,128)(2,1)} %param.15) | copy-start | bytes 3932164
  10.4 3.9 %copy-start.2 = (bf16[32,256,128]{2,1,0:T(8,128)(2,1)S(1)}, bf16[32,256,128]{2,1,0:T(8,128)(2,1)}, u32[]{:S(2)}) copy-start(bf16[32,256,128]{2,1,0:T(8,128)(2,1)} %param.13) | copy-start | bytes 6291460
  83.1 57.1 %all-to-all-start.1 = ((bf16[32,256,128]{2,1,0:T(8,128)(2,1)}), bf16[32,256,128]{2,1,0:T(8,128)(2,1)S(1)}, u32[]{:S(2)}, u32[]{:S(2)}) async-start(bf16[32,256,128]{2,1,0:T(8,128)(2,1)} %get-tuple-element.32), calls=%async_computation.1 | async-start | bytes 4194304 | tf_op jit(solution)/shard_map/all_to_all | solution.py:111
  89.4 4.6 %copy-start.6 = (s32[448]{0:T(512)S(1)}, s32[448]{0:T(512)}, u32[]{:S(2)}) copy-start(s32[448]{0:T(512)} %param.20) | copy-start | bytes 5380
  89.4 4.6 %copy-start.7 = (s32[448]{0:T(512)S(1)}, s32[448]{0:T(512)}, u32[]{:S(2)}) copy-start(s32[448]{0:T(512)} %param.21) | copy-start | bytes 5380
  89.4 106.2 %reduce-scatter.2.cloned.1.call-start = ((), (), s32[]{:S(2)}) async-start(), calls=%async_computation.3 | async-start | bytes 1474560 | tf_op jit(solution)/shard_map/reduce_scatter | solution.py:134
  98.1 3.1 %copy-start.1 = (s32[1024]{0:T(1024)S(1)}, s32[1024]{0:T(1024)}, u32[]{:S(2)}) copy-start(s32[1024]{0:T(1024)} %param.19) | copy-start | bytes 12292
  98.1 3.9 %copy-start.4 = (bf16[32,2,512]{2,1,0:T(2,128)(2,1)S(1)}, bf16[32,2,512]{2,1,0:T(2,128)(2,1)}, u32[]{:S(2)}) copy-start(bf16[32,2,512]{2,1,0:T(2,128)(2,1)} %param.12) | copy-start | bytes 196612
  98.1 4.6 %copy-start.9 = (f32[128]{0:T(128)S(1)}, f32[128]{0:T(128)}, u32[]{:S(2)}) copy-start(f32[128]{0:T(128)} %param.17) | copy-start | bytes 1540
  142.4 7.8 %copy-start.5 = (bf16[32,2,4,128]{3,2,1,0:T(4,128)(2,1)S(1)}, bf16[32,2,4,128]{3,2,1,0:T(4,128)(2,1)}, u32[]{:S(2)}) copy-start(bf16[32,2,4,128]{3,2,1,0:T(4,128)(2,1)} %reshape.288) | copy-start | bytes 196612
  150.2 4.2 %copy-start.3 = (bf16[32,256,128]{2,1,0:T(8,128)(2,1)}, bf16[32,256,128]{2,1,0:T(8,128)(2,1)S(1)}, u32[]{:S(2)}) copy-start(bf16[32,256,128]{2,1,0:T(8,128)(2,1)S(1)} %get-tuple-element.20) | copy-start | bytes 6291460
  152.3 2.2 %copy-start.8 = (pred[32]{0:T(512)(128)(4,1)S(1)}, pred[32]{0:T(512)(128)(4,1)}, u32[]{:S(2)}) copy-start(pred[32]{0:T(512)(128)(4,1)} %broadcast_compare_fusion.1) | copy-start | bytes 100
Sparse Core Ops, SparseCore 0:
  159.2 36.3 reduce-scatter.1
where the time goes:
time: 208 us; the launch traced here: 204 us
  waiting for transfers between devices  66.7 us (32%)
  blocking collectives  62.9 us (30%)
  local copies, waits for them, and re-layouts  23.5 us (11%)
  other arithmetic  18.2 us (9%)
  between operations  14.3 us (7%)
  matrix products  12.2 us (6%)
  starting transfers between devices  6.25 us (3%)
    all_to_all x1, blocking collectives, shards(): lax.all_to_all(pack_values, 'replica', split_axis=0, concat_axis=0, tiled...  62.9 us
    reduce_scatter x1, waiting for transfers between devices, shards(): lax.psum_scatter(head_terms, 'tensor', scatter_dimension=2, tiled=True)  36.5 us
    all_to_all x1, waiting for transfers between devices, shards(): lax.all_to_all(pack_keys, 'replica', split_axis=0, concat_axis=0, tiled=T...  30.2 us
    select_n x1, other arithmetic, place(): return jnp.where(active[:, None, None], kept, jnp.zeros_like(kept))  7.77 us
    all_to_all x1, starting transfers between devices, shards(): lax.all_to_all(pack_keys, 'replica', split_axis=0, concat_axis=0, tiled=T...  6.21 us
    scatter x2, local copies, waits for them, and re-layouts, shards(): anchor = all_slots.at[move_src].set(-1).at[move_dst].set(move_src)  5.83 us
    dot_general x1, matrix products, shards(): jnp.dot(mixture.reshape(local_count * 2, -1), out_weight, preferred_eleme...  4.58 us
  transfers between devices with their start and end apart: 2, of which 2 were waited for; matrix products, arithmetic and copies ran while one was open for 10% of the time, Pallas kernels for 0%

commit v1 on v0

v1 whole, which is shorter than its diff:
```python
import functools
import math

import jax
import jax.numpy as jnp
from jax import lax
from jax.experimental import pallas as pl
from jax.experimental.pallas import tpu as pltpu
from jax.sharding import PartitionSpec as P

EPS = 1e-06
THETA = 1000000.0
MESH = pl.DeviceIdType.MESH
MOVES = 14
STEP_ROWS = 24


def plan_kernel(slots, replicas, me_ref, len_ref, src_ref, dst_ref, send_ref, from_ref, live_ref, llen_ref, dead_ref, pos_ref, row_ref, found, mark, newlen):
    me = me_ref[0]
    kept_count = slots - 2 * MOVES

    def clear(i, _):
        mark[i] = -1
        newlen[i] = 0
        return 0

    lax.fori_loop(0, slots, clear, 0)

    def clear_sends(i, _):
        send_ref[i] = 0
        return 0

    lax.fori_loop(0, replicas, clear_sends, 0)

    def out(k, _):
        s, d = src_ref[me * MOVES + k], dst_ref[me * MOVES + k]
        mark[s % slots] = -2
        send_ref[(d // slots - me) % replicas] = s % slots
        return 0

    lax.fori_loop(0, MOVES, out, 0)

    def search(j, count):
        found[count] = j
        return count + jnp.where(dst_ref[j] // slots == me, 1, 0)

    lax.fori_loop(0, src_ref.shape[0], search, 0, unroll=8)

    def keep(s, count):
        length = len_ref[me * slots + s]
        stays = (mark[s] != -2) & (length > 0)
        live_ref[count] = s
        llen_ref[count] = length
        mark[s] = jnp.where(stays, count, -1)
        newlen[s] = jnp.where(stays, length, 0)
        return count + jnp.where(stays, 1, 0)

    lax.fori_loop(0, slots, keep, 0)

    def arrive(e, _):
        j = found[e]
        s, d = src_ref[j], dst_ref[j] % slots
        length = len_ref[s]
        from_ref[e] = (me - s // slots) % replicas
        live_ref[kept_count + e] = d
        llen_ref[kept_count + e] = length
        mark[d] = kept_count + e
        newlen[d] = length
        return 0

    lax.fori_loop(0, MOVES, arrive, 0)

    def finish(s, count):
        at = mark[s]
        dead_ref[count] = s
        for t in range(2):
            pos_ref[pl.ds(2 * s + t, 1), :] = jnp.full((1, 128), newlen[s] + t, jnp.int32).astype(jnp.float32)
            row_ref[pl.ds(2 * s + t, 1), :] = jnp.full((1, 128), jnp.where(at < 0, -1, at + t * STEP_ROWS), jnp.int32)
        return count + jnp.where(at < 0, 1, 0)

    lax.fori_loop(0, slots, finish, 0)


def plan(me, lengths, move_src, move_dst, slots, replicas):
    smem = pl.BlockSpec(memory_space=pltpu.SMEM)
    vmem = pl.BlockSpec(memory_space=pltpu.VMEM)
    ints = lambda n: jax.ShapeDtypeStruct((n,), jnp.int32)
    live = slots - MOVES
    return pl.pallas_call(
        functools.partial(plan_kernel, slots, replicas),
        out_shape=(
            ints(replicas),
            ints(MOVES),
            ints(live + 1),
            ints(live + 1),
            ints(MOVES + 1),
            jax.ShapeDtypeStruct((2 * slots, 128), jnp.float32),
            jax.ShapeDtypeStruct((2 * slots, 128), jnp.int32),
        ),
        in_specs=[smem] * 4,
        out_specs=(smem,) * 5 + (vmem,) * 2,
        scratch_shapes=[
            pltpu.SMEM((MOVES + 1,), jnp.int32),
            pltpu.SMEM((slots,), jnp.int32),
            pltpu.SMEM((slots,), jnp.int32),
        ],
    )(me, lengths, move_src, move_dst)


def layer_kernel(
    replicas,
    tensors,
    send_ref,
    from_ref,
    live_ref,
    llen_ref,
    pos_ref,
    row_ref,
    gain_ref,
    hidden_hbm,
    query_hbm,
    ck_hbm,
    cv_hbm,
    kw_hbm,
    vw_hbm,
    ow_hbm,
    branch_ref,
    list_hbm,
    ck,
    cv,
    hid,
    qry,
    kw,
    vw,
    ow,
    stage,
    recv,
    listed,
    fresh_k,
    fresh_v,
    mix,
    rs_stage,
    rs_recv,
    reduced,
    in_sem,
    send_sem,
    recv_sem,
    rs_send_sem,
    rs_recv_sem,
    list_sem,
):
    me = lax.axis_index("replica")
    at = lax.axis_index("tensor")
    slots, rows, width = ck.shape
    live = listed.shape[0]
    kept = live - MOVES
    groups = query_hbm.shape[2] // width

    loads = [
        pltpu.make_async_copy(source, target, in_sem.at[i])
        for i, (source, target) in enumerate(
            (
                (ck_hbm, ck),
                (cv_hbm, cv),
                (hidden_hbm, hid),
                (kw_hbm, kw),
                (vw_hbm, vw),
                (query_hbm, qry),
                (ow_hbm, ow),
            )
        )
    ]
    for load in loads:
        load.start()

    barrier = pltpu.get_barrier_semaphore()

    def greet(j, _):
        pl.semaphore_signal(barrier, inc=1, device_id={"replica": lax.rem(me + j, replicas)}, device_id_type=MESH)
        return 0

    lax.fori_loop(1, replicas, greet, 0)

    def greet_tensor(j, _):
        pl.semaphore_signal(barrier, inc=1, device_id={"tensor": lax.rem(at + j, tensors)}, device_id_type=MESH)
        return 0

    lax.fori_loop(1, tensors, greet_tensor, 0)
    pl.semaphore_wait(barrier, replicas - 1 + tensors - 1)

    loads[0].wait()
    loads[1].wait()

    def move(j):
        return pltpu.make_async_remote_copy(
            src_ref=stage.at[j],
            dst_ref=recv.at[j],
            send_sem=send_sem.at[j],
            recv_sem=recv_sem.at[j],
            device_id={"replica": lax.rem(me + j, replicas)},
            device_id_type=MESH,
        )

    def send(j, _):
        slot = send_ref[j]
        stage[j, :rows, :] = ck[slot]
        stage[j, rows:, :] = cv[slot]
        move(j).start()
        return 0

    lax.fori_loop(1, replicas, send, 0)

    loads[2].wait()
    loads[3].wait()
    loads[4].wait()
    raw_k = jnp.dot(hid[...], kw[...], preferred_element_type=jnp.float32)
    raw_v = jnp.dot(hid[...], vw[...], preferred_element_type=jnp.float32)
    mean_square = jnp.mean(raw_k * raw_k, axis=-1, keepdims=True)
    normed = raw_k * lax.rsqrt(mean_square + EPS) * gain_ref[...]
    lane = lax.broadcasted_iota(jnp.int32, (1, width), 1)
    half = width // 2
    index = jnp.where(lane < half, lane, lane - half).astype(jnp.float32)
    angles = pos_ref[...] * jnp.exp(index * (-2.0 * math.log(THETA) / width))
    turned = pltpu.roll(normed, half, 1)
    sine = jnp.sin(angles)
    rotated = normed * jnp.cos(angles) + turned * jnp.where(lane < half, -sine, sine)
    fresh_k[...] = rotated.astype(jnp.bfloat16).astype(jnp.float32)
    fresh_v[...] = raw_v.astype(jnp.bfloat16).astype(jnp.float32)
    loads[5].wait()

    row_ids = lax.broadcasted_iota(jnp.int32, (rows, width), 0)
    column_ids = lax.broadcasted_iota(jnp.int32, (2 * groups, rows), 1)
    step_ids = lax.broadcasted_iota(jnp.int32, (2 * groups, rows), 0) % 2

    def placed(stored, fresh, slot, length):
        full = jnp.where(row_ids < length, stored.astype(jnp.float32), 0.0)
        full = jnp.where(row_ids == length, fresh[pl.ds(2 * slot, 1), :], full)
        full = jnp.where(row_ids == length + 1, fresh[pl.ds(2 * slot + 1, 1), :], full)
        return full.astype(jnp.bfloat16)

    def attend(e, stored_k, stored_v):
        slot, length = live_ref[e], llen_ref[e]
        keys = placed(stored_k, fresh_k, slot, length)
        values = placed(stored_v, fresh_v, slot, length)
        listed[e, :rows, :] = keys
        listed[e, rows:, :] = values
        pltpu.make_async_copy(listed.at[e], list_hbm.at[e], list_sem.at[e]).start()
        q = qry[slot].astype(jnp.float32)
        q = jnp.concatenate([q[:, g * width : (g + 1) * width] for g in range(groups)], axis=0).astype(jnp.bfloat16)
        scores = lax.dot_general(q, keys, (((1,), (1,)), ((), ())), preferred_element_type=jnp.float32) * width ** (-0.5)
        scores = jnp.where(column_ids <= length + step_ids, scores, -jnp.inf)
        weights = jnp.exp(scores - jnp.max(scores, axis=-1, keepdims=True))
        shares = (weights / jnp.sum(weights, axis=-1, keepdims=True)).astype(jnp.bfloat16)
        mix[pl.ds(pl.multiple_of(e * 2 * groups, 2 * groups), 2 * groups), :] = jnp.dot(shares, values, preferred_element_type=jnp.float32)

    def attend_kept(e, _):
        slot = live_ref[e]
        attend(e, ck[slot], cv[slot])
        return 0

    lax.fori_loop(0, kept, attend_kept, 0)
    mix[2 * groups * live :, :] = jnp.zeros((mix.shape[0] - 2 * groups * live, width), jnp.float32)
    reduced[...] = jnp.zeros_like(reduced)
    loads[6].wait()

    def arrived(j, _):
        move(j).wait_recv()
        return 0

    lax.fori_loop(1, replicas, arrived, 0)

    def attend_arrived(i, _):
        source = from_ref[i]
        attend(kept + i, recv[source, :rows, :], recv[source, rows:, :])
        return 0

    lax.fori_loop(0, MOVES, attend_arrived, 0, unroll=2)

    steps = [
        jnp.concatenate([mix[pl.ds(2 * g + t, STEP_ROWS, stride=2 * groups), :] for g in range(groups)], axis=1)
        for t in range(2)
    ]
    mixture = jnp.concatenate(steps, axis=0).astype(jnp.bfloat16)
    out_width = branch_ref.shape[1]

    def part(j):
        first = pl.multiple_of(lax.rem(at + j, tensors) * out_width, 128)
        return jnp.dot(mixture, ow[:, pl.ds(first, out_width)], preferred_element_type=jnp.float32)

    def give(j):
        return pltpu.make_async_remote_copy(
            src_ref=rs_stage.at[j],
            dst_ref=rs_recv.at[j],
            send_sem=rs_send_sem.at[j],
            recv_sem=rs_recv_sem.at[j],
            device_id={"tensor": lax.rem(at + j, tensors)},
            device_id_type=MESH,
        )

    def give_part(j, _):
        rs_stage[j] = part(j).astype(jnp.bfloat16)
        give(j).start()
        return 0

    lax.fori_loop(1, tensors, give_part, 0)
    total = part(0)
    for j in range(1, tensors):
        give(j).wait_recv()
        total = total + rs_recv[j].astype(jnp.float32)
    reduced[: 2 * STEP_ROWS, :] = total.astype(jnp.bfloat16)
    pick = (lax.broadcasted_iota(jnp.int32, row_ref.shape, 1) == row_ref[...]).astype(jnp.float32).astype(jnp.bfloat16)
    branch_ref[...] = jnp.dot(pick, reduced[...], preferred_element_type=jnp.float32).astype(jnp.bfloat16)

    def sent(j, _):
        move(j).wait_send()
        return 0

    lax.fori_loop(1, replicas, sent, 0)

    def given(j, _):
        give(j).wait_send()
        return 0

    lax.fori_loop(1, tensors, given, 0)

    def written(e, _):
        pltpu.make_async_copy(listed.at[e], list_hbm.at[e], list_sem.at[e]).wait()
        return 0

    lax.fori_loop(0, live, written, 0)


def layer(replicas, tensors, scalars, rows_at, gain, hidden, queries, cache_keys, cache_values, key_weight, value_weight, out_weight):
    slots, rows, width = cache_keys.shape
    live = slots - MOVES
    groups = queries.shape[2] // width
    out_width = out_weight.shape[1] // tensors
    smem = pl.BlockSpec(memory_space=pltpu.SMEM)
    vmem = pl.BlockSpec(memory_space=pltpu.VMEM)
    any_ = pl.BlockSpec(memory_space=pl.ANY)
    bf16 = jnp.bfloat16
    dma = pltpu.SemaphoreType.DMA
    operands = (hidden, queries, cache_keys, cache_values, key_weight, value_weight, out_weight)
    return pl.pallas_call(
        functools.partial(layer_kernel, replicas, tensors),
        out_shape=(
            jax.ShapeDtypeStruct((2 * slots, out_width), bf16),
            jax.ShapeDtypeStruct((live, 2 * rows, width), bf16),
        ),
        in_specs=[smem] * 4 + [vmem] * 3 + [any_] * len(operands),
        out_specs=(vmem, any_),
        scratch_shapes=[
            pltpu.VMEM(cache_keys.shape, bf16),
            pltpu.VMEM(cache_values.shape, bf16),
            pltpu.VMEM(hidden.shape, bf16),
            pltpu.VMEM(queries.shape, bf16),
            pltpu.VMEM(key_weight.shape, bf16),
            pltpu.VMEM(value_weight.shape, bf16),
            pltpu.VMEM(out_weight.shape, bf16),
            pltpu.VMEM((replicas, 2 * rows, width), bf16),
            pltpu.VMEM((replicas, 2 * rows, width), bf16),
            pltpu.VMEM((live, 2 * rows, width), bf16),
            pltpu.VMEM((2 * slots, width), jnp.float32),
            pltpu.VMEM((2 * slots, width), jnp.float32),
            pltpu.VMEM((2 * groups * STEP_ROWS, width), jnp.float32),
            pltpu.VMEM((tensors, 2 * STEP_ROWS, out_width), bf16),
            pltpu.VMEM((tensors, 2 * STEP_ROWS, out_width), bf16),
            pltpu.VMEM((128, out_width), bf16),
            dma((len(operands),)),
            dma((replicas,)),
            dma((replicas,)),
            dma((tensors,)),
            dma((tensors,)),
            dma((live,)),
        ],
        compiler_params=pltpu.CompilerParams(
            collective_id=0, has_side_effects=True, vmem_limit_bytes=48 * 1024 * 1024
        ),
    )(*scalars, *rows_at, gain, *operands)


def place_kernel(live_ref, dead_ref, list_hbm, keys_hbm, values_hbm, zeros, sem):
    rows = zeros.shape[0]
    live = list_hbm.shape[0]
    zeros[...] = jnp.zeros_like(zeros)

    def copies(e):
        slot = live_ref[e]
        return (
            pltpu.make_async_copy(list_hbm.at[e, pl.ds(0, rows)], keys_hbm.at[slot], sem.at[e, 0]),
            pltpu.make_async_copy(list_hbm.at[e, pl.ds(rows, rows)], values_hbm.at[slot], sem.at[e, 1]),
        )

    def clears(e):
        slot = dead_ref[e]
        return (
            pltpu.make_async_copy(zeros, keys_hbm.at[slot], sem.at[live + e, 0]),
            pltpu.make_async_copy(zeros, values_hbm.at[slot], sem.at[live + e, 1]),
        )

    for act in ("start", "wait"):
        for make, count in ((copies, live), (clears, MOVES)):

            def each(e, _):
                for copy in make(e):
                    getattr(copy, act)()
                return 0

            lax.fori_loop(0, count, each, 0)


def place(live_slots, dead_slots, listed, slots):
    live, both, width = listed.shape
    shape = jax.ShapeDtypeStruct((slots, both // 2, width), listed.dtype)
    smem = pl.BlockSpec(memory_space=pltpu.SMEM)
    any_ = pl.BlockSpec(memory_space=pl.ANY)
    return pl.pallas_call(
        place_kernel,
        out_shape=(shape, shape),
        in_specs=[smem, smem, any_],
        out_specs=(any_, any_),
        scratch_shapes=[
            pltpu.VMEM((both // 2, width), listed.dtype),
            pltpu.SemaphoreType.DMA((slots, 2)),
        ],
    )(live_slots, dead_slots, listed)


def shards(hidden, queries, cache_keys, cache_values, key_weight, value_weight, key_gain, out_weight, lengths, move_src, move_dst):
    slots = cache_keys.shape[0]
    replicas, tensors = lax.axis_size("replica"), lax.axis_size("tensor")
    me = lax.axis_index("replica").astype(jnp.int32).reshape(1)
    send, source, live, llen, dead, pos, row = plan(me, lengths, move_src, move_dst, slots, replicas)
    branch, listed = layer(
        replicas,
        tensors,
        (send, source, live, llen),
        (pos, row),
        key_gain.reshape(1, -1),
        hidden.reshape(2 * slots, -1),
        queries,
        cache_keys,
        cache_values,
        key_weight,
        value_weight,
        out_weight,
    )
    keys_out, values_out = place(live, dead, listed, slots)
    return (branch.reshape(slots, 2, -1), keys_out, values_out)


def solution(mesh):
    placed = (
        P("replica", None, None),
        P("replica", None, "tensor"),
        P("replica", None, "tensor"),
        P("replica", None, "tensor"),
        P(None, "tensor"),
        P(None, "tensor"),
        P(),
        P("tensor", None),
        P(),
        P(),
        P(),
    )
    return jax.shard_map(
        shards,
        mesh=mesh,
        in_specs=placed,
        out_specs=(
            P("replica", None, "tensor"),
            P("replica", None, "tensor"),
            P("replica", None, "tensor"),
        ),
        check_vma=False,
    )
```

time: 208 us -> 218 us (1.048); the launches traced: 204 us -> 218 us
  Pallas kernels: 0 us -> 206 us
  waiting for transfers between devices: 66.7 us -> 0 us
  blocking collectives: 62.9 us -> 0 us
  other arithmetic: 18.2 us -> 0 us
  between operations: 14.3 us -> 0.69 us
  local copies, waits for them, and re-layouts: 23.5 us -> 11.2 us
  matrix products: 12.2 us -> 0 us
  starting transfers between devices: 6.25 us -> 0 us
    pallas_call x0 -> x3, Pallas kernels: none -> 206 us  [the longest x1 126 us: layer(): pl.pallas_call(functools.partial(layer_kernel, replicas, tensors), out_sh...]
    all_to_all x1 -> x0, blocking collectives: 62.9 us -> none  [shards(): lax.all_to_all(pack_values, 'replica', split_axis=0, concat_axis=0, tiled...]
    reduce_scatter x1 -> x0, waiting for transfers between devices: 36.5 us -> none  [shards(): lax.psum_scatter(head_terms, 'tensor', scatter_dimension=2, tiled=True)]
    all_to_all x1 -> x0, waiting for transfers between devices: 30.2 us -> none  [shards(): lax.all_to_all(pack_keys, 'replica', split_axis=0, concat_axis=0, tiled=T...]
    gather x5 -> x0, local copies, waits for them, and re-layouts: 12.5 us -> none  [the longest x1 3.87 us: shards(): cache_values[send_slot]]
    select_n x6 -> x0, other arithmetic: 12.4 us -> none  [the longest x1 7.77 us: place(): return jnp.where(active[:, None, None], kept, jnp.zeros_like(kept))]
    dot_general x4 -> x0, matrix products: 10.1 us -> none  [the longest x1 4.58 us: shards(): jnp.dot(mixture.reshape(local_count * 2, -1), out_weight, preferred_eleme...]
    unnamed x21 -> x22, local copies, waits for them, and re-layouts: 0.76 us -> 8.41 us
  transfers between devices with their start and end apart: 2 -> 0, of which waited for: 2 -> 0; matrix products, arithmetic and copies ran while one was open for 10% -> 0% of each run, Pallas kernels for 0% -> 0%
where the time goes in v1:
time: 218 us
  Pallas kernels  206 us (94%)
  local copies, waits for them, and re-layouts  11.2 us (5%)
    pallas_call x1, Pallas kernels, layer(): pl.pallas_call(functools.partial(layer_kernel, replicas, tensors), out_sh...  126 us
    pallas_call x1, Pallas kernels, place(): pl.pallas_call(place_kernel, out_shape=(shape, shape), in_specs=[smem, sm...  73.9 us
    unnamed x22, local copies, waits for them, and re-layouts  8.41 us
    pallas_call x1, Pallas kernels, plan(): pl.pallas_call(functools.partial(plan_kernel, slots, replicas), out_shape...  6.23 us

profile of v1, /device:TPU:1, one launch (start us, length us, event | category | flops | bytes accessed | tf_op | source)
XLA Modules:
  0.0 218.0 jit_solution(5481229197799821429)
XLA Ops:
  0.6 0.0 copy-start.1
  0.6 6.2 %shard_map.130 = (s32[32]{0:T(128)}, s32[14]{0:T(128)}, s32[19]{0:T(128)}, s32[19]{0:T(128)}, s32[15]{0:T(128)}, /*index=5*/f32[64,128]{1,0:T(8,128)}, s32[64,128]{1,0:T(8,128)}) custom-call(s32[1]{0:T(128)} %bitcast.me_ref, s32[1024]{0:T(1024)} %len_ref.1, s32[448]{0:T(512)} %src_ref.1, s32[448]{0:T(512)} %dst_ref.1), custom_call_target="tpu_custom_call" | custom-call | tf_op jit(solution)/shard_map/pallas_call | solution.py:89
  6.9 2.1 reshape.20.hidden_hbm
  9.0 0.0 copy-done.1
  9.0 0.0 copy-start
  9.0 1.6 copy-done
  10.6 0.0 copy-start.2
  10.6 1.3 copy-done.2
  11.9 0.0 copy-start.3
  11.9 0.8 copy-done.3
  12.7 0.0 copy-start.4
  12.7 0.8 copy-done.4
  13.5 0.0 copy-start.5
  13.5 0.8 copy-done.5
  14.3 0.0 copy-start.6
  14.3 0.6 copy-done.6
  14.9 0.0 copy-start.7
  14.9 0.7 copy-done.7
  15.5 0.0 copy-start.8
  15.5 0.6 copy-done.8
  16.1 0.0 copy-start.9
  16.1 0.6 copy-done.9
  16.8 0.0 copy-start.10
  16.8 0.7 copy-done.10
  17.4 126.0 %shard_map.131 = (bf16[64,640]{1,0:T(8,128)(2,1)S(1)}, bf16[18,512,128]{2,1,0:T(8,128)(2,1)}) custom-call(s32[32]{0:T(128)S(1)} %copy-done.8, s32[14]{0:T(128)S(1)} %copy-done.9, s32[19]{0:T(128)S(1)} %copy-done.6, s32[19]{0:T(128)S(1)} %copy-done.10, f32[64,128]{1,0:T(8,128)S(1)} %copy-done.4, s32[64,128]{1,0:T(8,128)S(1)} %copy-done.5, ...), custom_call_target="tpu_custom_call" | custom-call | tf_op jit(solution)/shard_map/pallas_call | solution.py:344
  143.5 0.7 reshape.21
  144.1 73.9 %shard_map.132 = (bf16[32,256,128]{2,1,0:T(8,128)(2,1)}, bf16[32,256,128]{2,1,0:T(8,128)(2,1)}) custom-call(s32[19]{0:T(128)} %get-tuple-element.16.live_ref, s32[15]{0:T(128)} %get-tuple-element.21.dead_ref, bf16[18,512,128]{2,1,0:T(8,128)(2,1)} %get-tuple-element.22.list_hbm), custom_call_target="tpu_custom_call" | custom-call | tf_op jit(solution)/shard_map/pallas_call | solution.py:417
Async XLA Ops:
  0.6 8.4 %copy-start.1 = (bf16[5120,128]{1,0:T(8,128)(2,1)S(1)}, bf16[5120,128]{1,0:T(8,128)(2,1)}, u32[]{:S(2)}) copy-start(bf16[5120,128]{1,0:T(8,128)(2,1)} %kw_hbm.1) | copy-start | bytes 3932164
  9.0 1.6 copy-start
  10.6 1.3 copy-start.2
  11.9 0.8 copy-start.3
  12.7 0.8 copy-start.4
  13.5 0.8 copy-start.5
  14.3 0.6 copy-start.6
  14.9 0.7 copy-start.7
  15.5 0.6 copy-start.8
  16.1 0.6 copy-start.9
  16.8 0.7 copy-start.10

commit v2 on v1

v2 whole, which is shorter than its diff:
```python
import functools
import math

import jax
import jax.numpy as jnp
from jax import lax
from jax.experimental import pallas as pl
from jax.experimental.pallas import tpu as pltpu
from jax.sharding import PartitionSpec as P

EPS = 1e-06
THETA = 1000000.0
MESH = pl.DeviceIdType.MESH
VMEM_LIMIT = 60 * 1024 * 1024
MOVES = 14
STEP_ROWS = 24
TIERS = (((7, 5, 3, 2), 10), ((8, 6, 4, 2), 11), ((10, 8, 5, 3), 14))


def route(me, lengths, move_src, move_dst, slots, replicas):
    ring = replicas // 4
    count = move_src.shape[0]
    order = jnp.arange(count, dtype=jnp.int32)
    from_rep, to_rep = move_src // slots, move_dst // slots
    ys, zs, cs = from_rep // (2 * ring), (from_rep // 2) % ring, from_rep % 2
    yd, zd = to_rep // (2 * ring), (to_rep // 2) % ring
    ahead = (zd - zs) % ring
    half = ring // 2
    group = (yd * ring + zs) * 2 + cs
    same = group[:, None] == group[None, :]
    before = order[None, :] < order[:, None]
    distance = jnp.where(ahead <= half, ahead, ring - ahead)
    pull = jnp.where(ahead == half, 0, jnp.where(ahead < half, ahead, ahead - ring))
    lean = jnp.sum(jnp.where(same, pull[None, :], 0), axis=1)
    rank_far = jnp.sum(same & before & (ahead == half)[None, :], axis=1, dtype=jnp.int32)
    way = jnp.where(ahead < half, 0, 1)
    for i in range(4):
        back = lean > 0
        way = jnp.where((ahead == half) & (rank_far == i), back.astype(jnp.int32), way)
        lean = lean + jnp.where(back, -half, half)
    travels = ahead != 0
    sort_key = jnp.where(travels, (group * 2 + way) * 8 - distance, -1)
    same_way = (sort_key[:, None] + 7) // 8 == (sort_key[None, :] + 7) // 8
    lower = (sort_key[None, :] < sort_key[:, None]) | ((sort_key[None, :] == sort_key[:, None]) & before)
    place_in = jnp.sum(same_way & lower & travels[None, :], axis=1, dtype=jnp.int32)
    spot = 2 * place_in + way
    crosses = travels & (ys != yd)
    y_key = jnp.where(crosses, from_rep * 64 + spot, -1)
    y_rank = jnp.sum(
        (from_rep[None, :] == from_rep[:, None]) & crosses[None, :] & (y_key[None, :] < y_key[:, None]), axis=1, dtype=jnp.int32
    )

    def fits(caps, y_cap):
        reach = sum((place_in < c).astype(jnp.int32) for c in caps)
        return jnp.all(~travels | ((distance <= reach) & (~crosses | (y_rank < y_cap))))

    tier = jnp.int32(len(TIERS))
    for i, (caps, y_cap) in reversed(list(enumerate(TIERS))):
        tier = jnp.where(fits(caps, y_cap), i, tier)

    my_y, my_z, my_c = me // (2 * ring), (me // 2) % ring, me % 2
    mine = from_rep == me
    in_group = travels & (group == (my_y * ring + my_z) * 2 + my_c)
    kind = jnp.where(ys == yd, 0, jnp.where(cs == to_rep % 2, 1, 2))
    spot_code = jnp.where(mine, move_src % slots, slots + y_rank)
    address = jnp.where(
        in_group,
        jnp.where(spot < 32, spot, -1),
        jnp.where(
            mine,
            jnp.where(travels, jnp.where(y_rank < 16, 32 + y_rank, -1), 48 + kind),
            jnp.where(to_rep == me, 64 + move_dst % slots, -1),
        ),
    )
    code = (((place_in * 2 + way) * 8 + distance) * 4 + kind) * 1024 + move_src + 1
    value = jnp.where(in_group, spot_code, jnp.where(mine, move_src % slots, code))
    wanted = jnp.arange(64 + slots, dtype=jnp.int32)
    table = jnp.sum(jnp.where(wanted[:, None] == address[None, :], value[None, :], 0), axis=1)
    return tier, table


SEND, INJECT, ACROSS, NEAR, LIVE, LENGTH, SOURCE, LANE, SPOT, KIND, TABLE = 0, 32, 64, 80, 96, 128, 160, 176, 192, 208, 224


def plan_kernel(slots, replicas, me_ref, len_ref, src_ref, dst_ref, table_ref, dead_ref, out_ref, row_ref, mark):
    me = me_ref[0]

    def clear(i, _):
        mark[i] = 0
        out_ref[SEND + i] = 0
        return 0

    lax.fori_loop(0, slots, clear, 0, unroll=8)

    def out(k, _):
        s, d = src_ref[me * MOVES + k], dst_ref[me * MOVES + k]
        mark[s % slots] = 1
        out_ref[SEND + (d // slots - me) % replicas] = s % slots
        return 0

    lax.fori_loop(0, MOVES, out, 0, unroll=2)

    def copy(i, _):
        out_ref[INJECT + i] = table_ref[i]
        return 0

    lax.fori_loop(0, 64, copy, 0, unroll=8)

    def each(s, counts):
        kept_count, in_count, dead_count = counts
        code = table_ref[64 + s]
        incoming = code > 0
        source = jnp.where(incoming, (code - 1) % 1024, me * slots + s)
        length = len_ref[source]
        stays = jnp.logical_not(incoming) & (mark[s] == 0) & (length > 0)
        alive = incoming | stays
        length = jnp.where(alive, length, 0)
        at = jnp.where(incoming, slots - 2 * MOVES + in_count, kept_count)
        where = jnp.where(alive, at, slots - 1)
        out_ref[LIVE + where] = s
        out_ref[LENGTH + where] = length
        dead_ref[dead_count] = s
        rest = (code - 1) // 1024
        kind = rest % 4
        distance = (rest // 4) % 8
        way = (rest // 32) % 2
        source_rep = source // slots
        slot_in = jnp.where(incoming, in_count, MOVES)
        out_ref[SOURCE + slot_in] = (me - source_rep) % replicas
        other_core = jnp.where(source_rep % 2 == me % 2, 0, 1)
        out_ref[LANE + slot_in] = (other_core * 2 + way) * 4 + distance - 1
        out_ref[SPOT + slot_in] = rest // 64
        out_ref[KIND + slot_in] = jnp.where(distance == 0, kind, -1)
        for t in range(2):
            row_ref[pl.ds(2 * s + t, 1), :] = jnp.full((1, 128), length + t, jnp.int32).astype(jnp.float32)
            row_ref[pl.ds(2 * (slots + s) + t, 1), :] = jnp.full(
                (1, 128), jnp.where(alive, at + t * STEP_ROWS, -1), jnp.int32
            ).astype(jnp.float32)
        one = jnp.int32(1)
        return (
            kept_count + jnp.where(stays, one, 0),
            in_count + jnp.where(incoming, one, 0),
            dead_count + jnp.where(alive, 0, one),
        )

    zero = jnp.int32(0)
    lax.fori_loop(0, slots, each, (zero, zero, zero))


def plan(me, lengths, move_src, move_dst, table, slots, replicas):
    smem = pl.BlockSpec(memory_space=pltpu.SMEM)
    vmem = pl.BlockSpec(memory_space=pltpu.VMEM)
    ints = lambda n: jax.ShapeDtypeStruct((n,), jnp.int32)
    return pl.pallas_call(
        functools.partial(plan_kernel, slots, replicas),
        out_shape=(ints(slots + 1), ints(TABLE), jax.ShapeDtypeStruct((4 * slots, 128), jnp.float32)),
        in_specs=[smem] * 5,
        out_specs=(smem, smem, vmem),
        scratch_shapes=[pltpu.SMEM((slots,), jnp.int32)],
    )(me, lengths, move_src, move_dst, table)


def timetable(caps, y_cap):
    ready = [(min(i, y_cap - 1) + 2.0, 0, "inject", i % 2, 1, i // 2) for i in range(2 * caps[0])]
    free = [0.0, 0.0]
    events = []
    while ready:
        ready.sort()
        event = ready.pop(0)
        events.append(event[2:])
        time, _, what, way, hop, spot = event
        if what == "inject" or (hop < len(caps) and spot < caps[hop]):
            free[way] = max(free[way], time) + 1.0
            onward = hop if what == "inject" else hop + 1
            ready.append((free[way] + 0.5, 1, "pass", way, onward, spot))
    return events


class Direct:
    def __init__(self, replicas, me, scalars, caches, stage, arrived, send_sem, recv_sem):
        self.replicas, self.me, self.scalars, self.caches = replicas, me, scalars, caches
        self.stage, self.arrived, self.send_sem, self.recv_sem = stage, arrived, send_sem, recv_sem
        self.partners = replicas - 1

    def each(self, act):
        def step(j, _):
            act(j)
            return 0

        lax.fori_loop(1, self.replicas, step, 0)

    def peer(self, j):
        return {"replica": lax.rem(self.me + j, self.replicas)}

    def greet(self, barrier):
        self.each(lambda j: pl.semaphore_signal(barrier, inc=1, device_id=self.peer(j), device_id_type=MESH))

    def move(self, j):
        return pltpu.make_async_remote_copy(
            src_ref=self.stage.at[j],
            dst_ref=self.arrived.at[j],
            send_sem=self.send_sem.at[j],
            recv_sem=self.recv_sem.at[j],
            device_id=self.peer(j),
            device_id_type=MESH,
        )

    def start(self):
        rows = self.caches[0].shape[1]

        def send(j):
            slot = self.scalars[SEND + j]
            self.stage[j, :rows, :] = self.caches[0][slot]
            self.stage[j, rows:, :] = self.caches[1][slot]
            self.move(j).start()

        self.each(send)

    def carry(self):
        self.each(lambda j: self.move(j).wait_recv())

    def where(self, i):
        return self.scalars[SOURCE + i]

    def finish(self):
        self.each(lambda j: self.move(j).wait_send())


class Ring:
    def __init__(self, tier, replicas, me, scalars, caches, arrived, inject, across, across_in, near, *sems):
        self.caps, self.y_cap = tier
        self.me, self.scalars, self.caches = me, scalars, caches
        self.arrived, self.inject, self.across, self.across_in, self.near = arrived, inject, across, across_in, near
        self.hop_send, self.hop_recv, self.core_send, self.core_recv, self.y_send, self.y_recv, self.near_send, self.near_recv = sems
        half = replicas // 2
        line = (me // half) * half
        ahead = line + lax.rem(me - line + 2, half)
        behind = line + lax.rem(me - line + half - 2, half)
        core = me + 1 - 2 * lax.rem(me, 2)
        opposite = lax.rem(me + half, replicas)
        both = lax.rem(core + half, replicas)
        self.ways = (ahead, behind)
        self.core, self.opposite = core, opposite
        self.near_peers = (core, opposite, both)
        self.partners = 5
        self.events = timetable(self.caps, self.y_cap)
        self.lanes = 2 * len(self.caps) * self.caps[0]

    def greet(self, barrier):
        for peer in self.ways + self.near_peers:
            pl.semaphore_signal(barrier, inc=1, device_id={"replica": peer}, device_id_type=MESH)

    def copy(self, source, target, send_sem, recv_sem, peer):
        return pltpu.make_async_remote_copy(
            src_ref=source, dst_ref=target, send_sem=send_sem, recv_sem=recv_sem, device_id={"replica": peer}, device_id_type=MESH
        )

    def lane(self, way, hop, spot):
        return (way * len(self.caps) + hop - 1) * self.caps[0] + spot

    def cross(self, b):
        return self.copy(self.across.at[b], self.across_in.at[b], self.y_send.at[b], self.y_recv.at[b], self.opposite)

    def next_door(self, j):
        target = self.arrived.at[2 * self.lanes + j]
        return self.copy(self.near.at[j], target, self.near_send.at[j], self.near_recv.at[j], self.near_peers[j])

    def hop(self, way, hop, spot):
        source = self.inject.at[2 * spot + way] if hop == 1 else self.arrived.at[self.lane(way, hop - 1, spot)]
        to = self.lane(way, hop, spot)
        return self.copy(source, self.arrived.at[to], self.hop_send.at[to], self.hop_recv.at[to], self.ways[way])

    def hand_over(self, way, hop, spot):
        at = self.lane(way, hop, spot)
        return self.copy(
            self.arrived.at[at], self.arrived.at[self.lanes + at], self.core_send.at[at], self.core_recv.at[at], self.core
        )

    def pack(self, target, at, slot):
        rows = self.caches[0].shape[1]
        target[at, :rows, :] = self.caches[0][slot]
        target[at, rows:, :] = self.caches[1][slot]

    def start(self):
        for b in range(self.y_cap):
            self.pack(self.across, b, self.scalars[ACROSS + b])
            self.cross(b).start()
        for j in range(3):
            self.pack(self.near, j, self.scalars[NEAR + j])
            self.next_door(j).start()

    def carry(self):
        slots, rows, _ = self.caches[0].shape
        crossed = 0
        for what, way, hop, spot in self.events:
            if what == "inject":
                i = 2 * spot + way
                while crossed < min(i + 1, self.y_cap):
                    self.cross(crossed).wait_recv()
                    crossed += 1
                code = self.scalars[INJECT + i]
                slot = jnp.where(code < slots, code, 0)
                for part in range(2):
                    block = self.caches[part][slot]
                    for b in range(crossed):
                        block = jnp.where(code == slots + b, self.across_in[b, part * rows : (part + 1) * rows, :], block)
                    self.inject[i, part * rows : (part + 1) * rows, :] = block
                self.hop(way, 1, spot).start()
            else:
                self.hop(way, hop, spot).wait_recv()
                if hop < len(self.caps) and spot < self.caps[hop]:
                    self.hop(way, hop + 1, spot).start()
                self.hand_over(way, hop, spot).start()
        for j in range(3):
            self.next_door(j).wait_recv()
        for what, way, hop, spot in self.events:
            if what == "pass":
                self.hand_over(way, hop, spot).wait_recv()

    def where(self, i):
        kind = self.scalars[KIND + i]
        return jnp.where(kind >= 0, 2 * self.lanes + kind, self.scalars[LANE + i] * self.caps[0] + self.scalars[SPOT + i])

    def finish(self):
        for b in range(self.y_cap):
            self.cross(b).wait_send()
        for j in range(3):
            self.next_door(j).wait_send()
        for what, way, hop, spot in self.events:
            if what == "pass":
                self.hop(way, hop, spot).wait_send()
                self.hand_over(way, hop, spot).wait_send()


def layer_kernel(
    replicas,
    tensors,
    tier,
    scalar_ref,
    row_ref,
    gain_ref,
    hidden_hbm,
    query_hbm,
    ck_hbm,
    cv_hbm,
    kw_hbm,
    vw_hbm,
    ow_hbm,
    branch_ref,
    list_hbm,
    ck,
    cv,
    hid,
    qry,
    kw,
    vw,
    ow,
    listed,
    fresh_k,
    fresh_v,
    mix,
    rs_stage,
    rs_recv,
    reduced,
    in_sem,
    rs_send_sem,
    rs_recv_sem,
    list_sem,
    *transport,
):
    me = lax.axis_index("replica")
    at = lax.axis_index("tensor")
    slots, rows, width = ck.shape
    live = listed.shape[0]
    kept = live - MOVES
    groups = query_hbm.shape[2] // width

    loads = [
        pltpu.make_async_copy(source, target, in_sem.at[i])
        for i, (source, target) in enumerate(
            (
                (ck_hbm, ck),
                (cv_hbm, cv),
                (hidden_hbm, hid),
                (kw_hbm, kw),
                (vw_hbm, vw),
                (query_hbm, qry),
                (ow_hbm, ow),
            )
        )
    ]
    for load in loads:
        load.start()

    caches = (ck, cv)
    if tier is None:
        road = Direct(replicas, me, scalar_ref, caches, *transport)
    else:
        road = Ring(tier, replicas, me, scalar_ref, caches, *transport)

    barrier = pltpu.get_barrier_semaphore()
    road.greet(barrier)

    def greet_tensor(j, _):
        pl.semaphore_signal(barrier, inc=1, device_id={"tensor": lax.rem(at + j, tensors)}, device_id_type=MESH)
        return 0

    lax.fori_loop(1, tensors, greet_tensor, 0)
    pl.semaphore_wait(barrier, road.partners + tensors - 1)

    loads[0].wait()
    loads[1].wait()
    road.start()

    loads[2].wait()
    loads[3].wait()
    loads[4].wait()
    raw_k = jnp.dot(hid[...], kw[...], preferred_element_type=jnp.float32)
    raw_v = jnp.dot(hid[...], vw[...], preferred_element_type=jnp.float32)
    mean_square = jnp.mean(raw_k * raw_k, axis=-1, keepdims=True)
    normed = raw_k * lax.rsqrt(mean_square + EPS) * gain_ref[...]
    lane = lax.broadcasted_iota(jnp.int32, (1, width), 1)
    half = width // 2
    index = jnp.where(lane < half, lane, lane - half).astype(jnp.float32)
    angles = row_ref[: 2 * slots, :] * jnp.exp(index * (-2.0 * math.log(THETA) / width))
    turned = pltpu.roll(normed, half, 1)
    sine = jnp.sin(angles)
    rotated = normed * jnp.cos(angles) + turned * jnp.where(lane < half, -sine, sine)
    fresh_k[...] = rotated.astype(jnp.bfloat16).astype(jnp.float32)
    fresh_v[...] = raw_v.astype(jnp.bfloat16).astype(jnp.float32)
    loads[5].wait()

    row_ids = lax.broadcasted_iota(jnp.int32, (rows, width), 0)
    column_ids = lax.broadcasted_iota(jnp.int32, (2 * groups, rows), 1)
    step_ids = lax.broadcasted_iota(jnp.int32, (2 * groups, rows), 0) % 2

    def placed(stored, fresh, slot, length):
        full = jnp.where(row_ids < length, stored.astype(jnp.float32), 0.0)
        full = jnp.where(row_ids == length, fresh[pl.ds(2 * slot, 1), :], full)
        full = jnp.where(row_ids == length + 1, fresh[pl.ds(2 * slot + 1, 1), :], full)
        return full.astype(jnp.bfloat16)

    def attend(e, stored_k, stored_v):
        slot, length = scalar_ref[LIVE + e], scalar_ref[LENGTH + e]
        keys = placed(stored_k, fresh_k, slot, length)
        values = placed(stored_v, fresh_v, slot, length)
        listed[e, :rows, :] = keys
        listed[e, rows:, :] = values
        pltpu.make_async_copy(listed.at[e], list_hbm.at[e], list_sem.at[e]).start()
        q = qry[slot].astype(jnp.float32)
        q = jnp.concatenate([q[:, g * width : (g + 1) * width] for g in range(groups)], axis=0).astype(jnp.bfloat16)
        scores = lax.dot_general(q, keys, (((1,), (1,)), ((), ())), preferred_element_type=jnp.float32) * width ** (-0.5)
        scores = jnp.where(column_ids <= length + step_ids, scores, -jnp.inf)
        weights = jnp.exp(scores - jnp.max(scores, axis=-1, keepdims=True))
        shares = (weights / jnp.sum(weights, axis=-1, keepdims=True)).astype(jnp.bfloat16)
        mix[pl.ds(pl.multiple_of(e * 2 * groups, 2 * groups), 2 * groups), :] = jnp.dot(shares, values, preferred_element_type=jnp.float32)

    def attend_kept(e, _):
        slot = scalar_ref[LIVE + e]
        attend(e, ck[slot], cv[slot])
        return 0

    lax.fori_loop(0, kept, attend_kept, 0)
    mix[2 * groups * live :, :] = jnp.zeros((mix.shape[0] - 2 * groups * live, width), jnp.float32)
    reduced[...] = jnp.zeros_like(reduced)
    loads[6].wait()

    road.carry()

    def attend_arrived(i, _):
        source = road.where(i)
        attend(kept + i, road.arrived[source, :rows, :], road.arrived[source, rows:, :])
        return 0

    lax.fori_loop(0, MOVES, attend_arrived, 0, unroll=2)

    steps = [
        jnp.concatenate([mix[pl.ds(2 * g + t, STEP_ROWS, stride=2 * groups), :] for g in range(groups)], axis=1)
        for t in range(2)
    ]
    mixture = jnp.concatenate(steps, axis=0).astype(jnp.bfloat16)
    out_width = branch_ref.shape[1]

    def part(j):
        first = pl.multiple_of(lax.rem(at + j, tensors) * out_width, 128)
        return jnp.dot(mixture, ow[:, pl.ds(first, out_width)], preferred_element_type=jnp.float32)

    def give(j):
        return pltpu.make_async_remote_copy(
            src_ref=rs_stage.at[j],
            dst_ref=rs_recv.at[j],
            send_sem=rs_send_sem.at[j],
            recv_sem=rs_recv_sem.at[j],
            device_id={"tensor": lax.rem(at + j, tensors)},
            device_id_type=MESH,
        )

    def give_part(j, _):
        rs_stage[j] = part(j).astype(jnp.bfloat16)
        give(j).start()
        return 0

    lax.fori_loop(1, tensors, give_part, 0)
    total = part(0)
    for j in range(1, tensors):
        give(j).wait_recv()
        total = total + rs_recv[j].astype(jnp.float32)
    reduced[: 2 * STEP_ROWS, :] = total.astype(jnp.bfloat16)
    rows_at = row_ref[2 * slots :, :]
    pick = (lane.astype(jnp.float32) == rows_at).astype(jnp.float32).astype(jnp.bfloat16)
    branch_ref[...] = jnp.dot(pick, reduced[...], preferred_element_type=jnp.float32).astype(jnp.bfloat16)

    road.finish()

    def given(j, _):
        give(j).wait_send()
        return 0

    lax.fori_loop(1, tensors, given, 0)

    def written(e, _):
        pltpu.make_async_copy(listed.at[e], list_hbm.at[e], list_sem.at[e]).wait()
        return 0

    lax.fori_loop(0, live, written, 0)


def layer(tier, replicas, tensors, scalars, rows_at, gain, *operands):
    hidden, queries, cache_keys, cache_values, key_weight, value_weight, out_weight = operands
    slots, rows, width = cache_keys.shape
    live = slots - MOVES
    groups = queries.shape[2] // width
    out_width = out_weight.shape[1] // tensors
    smem = pl.BlockSpec(memory_space=pltpu.SMEM)
    vmem = pl.BlockSpec(memory_space=pltpu.VMEM)
    any_ = pl.BlockSpec(memory_space=pl.ANY)
    bf16 = jnp.bfloat16
    dma = pltpu.SemaphoreType.DMA

    def rollouts(n):
        return pltpu.VMEM((n, 2 * rows, width), bf16)

    if tier is None:
        transport = [rollouts(replicas), rollouts(replicas), dma((replicas,)), dma((replicas,))]
    else:
        caps, y_cap = tier
        lanes = 2 * len(caps) * caps[0]
        transport = [
            rollouts(2 * lanes + 3),
            rollouts(2 * caps[0]),
            rollouts(y_cap),
            rollouts(y_cap),
            rollouts(3),
        ] + [dma((n,)) for n in (lanes, lanes, lanes, lanes, y_cap, y_cap, 3, 3)]
    return pl.pallas_call(
        functools.partial(layer_kernel, replicas, tensors, tier),
        out_shape=(
            jax.ShapeDtypeStruct((2 * slots, out_width), bf16),
            jax.ShapeDtypeStruct((live, 2 * rows, width), bf16),
        ),
        in_specs=[smem] + [vmem] * 2 + [any_] * len(operands),
        out_specs=(vmem, any_),
        scratch_shapes=[
            pltpu.VMEM(cache_keys.shape, bf16),
            pltpu.VMEM(cache_values.shape, bf16),
            pltpu.VMEM(hidden.shape, bf16),
            pltpu.VMEM(queries.shape, bf16),
            pltpu.VMEM(key_weight.shape, bf16),
            pltpu.VMEM(value_weight.shape, bf16),
            pltpu.VMEM(out_weight.shape, bf16),
            pltpu.VMEM((live, 2 * rows, width), bf16),
            pltpu.VMEM((2 * slots, width), jnp.float32),
            pltpu.VMEM((2 * slots, width), jnp.float32),
            pltpu.VMEM((2 * groups * STEP_ROWS, width), jnp.float32),
            pltpu.VMEM((tensors, 2 * STEP_ROWS, out_width), bf16),
            pltpu.VMEM((tensors, 2 * STEP_ROWS, out_width), bf16),
            pltpu.VMEM((128, out_width), bf16),
            dma((len(operands),)),
            dma((tensors,)),
            dma((tensors,)),
            dma((live,)),
        ]
        + transport,
        compiler_params=pltpu.CompilerParams(
            collective_id=len(TIERS) if tier is None else TIERS.index(tier),
            has_side_effects=True,
            vmem_limit_bytes=VMEM_LIMIT,
        ),
    )(scalars, rows_at, gain, *operands)


def place_kernel(scalar_ref, dead_ref, list_hbm, keys_hbm, values_hbm, listed, zeros, sem):
    rows = zeros.shape[0]
    live = listed.shape[0]
    load = pltpu.make_async_copy(list_hbm, listed, sem.at[live + MOVES, 0])
    load.start()
    zeros[...] = jnp.zeros_like(zeros)

    def copies(e):
        slot = scalar_ref[LIVE + e]
        return (
            pltpu.make_async_copy(listed.at[e, pl.ds(0, rows)], keys_hbm.at[slot], sem.at[e, 0]),
            pltpu.make_async_copy(listed.at[e, pl.ds(rows, rows)], values_hbm.at[slot], sem.at[e, 1]),
        )

    def clears(e):
        slot = dead_ref[e]
        return (
            pltpu.make_async_copy(zeros, keys_hbm.at[slot], sem.at[live + e, 0]),
            pltpu.make_async_copy(zeros, values_hbm.at[slot], sem.at[live + e, 1]),
        )

    def run(make, count, act):
        def each(e, _):
            for copy in make(e):
                getattr(copy, act)()
            return 0

        lax.fori_loop(0, count, each, 0)

    run(clears, MOVES, "start")
    load.wait()
    run(copies, live, "start")
    run(clears, MOVES, "wait")
    run(copies, live, "wait")


def place(scalars, dead_slots, listed, slots):
    live, both, width = listed.shape
    shape = jax.ShapeDtypeStruct((slots, both // 2, width), listed.dtype)
    smem = pl.BlockSpec(memory_space=pltpu.SMEM)
    any_ = pl.BlockSpec(memory_space=pl.ANY)
    return pl.pallas_call(
        place_kernel,
        out_shape=(shape, shape),
        in_specs=[smem, smem, any_],
        out_specs=(any_, any_),
        scratch_shapes=[
            pltpu.VMEM(listed.shape, listed.dtype),
            pltpu.VMEM((both // 2, width), listed.dtype),
            pltpu.SemaphoreType.DMA((slots + 1, 2)),
        ],
    )(scalars, dead_slots, listed)


def shards(hidden, queries, cache_keys, cache_values, key_weight, value_weight, key_gain, out_weight, lengths, move_src, move_dst):
    slots = cache_keys.shape[0]
    replicas, tensors = lax.axis_size("replica"), lax.axis_size("tensor")
    me = lax.axis_index("replica").astype(jnp.int32)
    tier, table = route(me, lengths, move_src, move_dst, slots, replicas)
    dead, scalars, rows_at = plan(me.reshape(1), lengths, move_src, move_dst, table, slots, replicas)
    operands = (
        scalars,
        rows_at,
        key_gain.reshape(1, -1),
        hidden.reshape(2 * slots, -1),
        queries,
        cache_keys,
        cache_values,
        key_weight,
        value_weight,
        out_weight,
    )
    branches = [functools.partial(layer, t, replicas, tensors) for t in TIERS + (None,)]
    branch, listed = lax.switch(tier, branches, *operands)
    keys_out, values_out = place(scalars, dead, listed, slots)
    return (branch.reshape(slots, 2, -1), keys_out, values_out)


def solution(mesh):
    placed = (
        P("replica", None, None),
        P("replica", None, "tensor"),
        P("replica", None, "tensor"),
        P("replica", None, "tensor"),
        P(None, "tensor"),
        P(None, "tensor"),
        P(),
        P("tensor", None),
        P(),
        P(),
        P(),
    )
    return jax.shard_map(
        shards,
        mesh=mesh,
        in_specs=placed,
        out_specs=(
            P("replica", None, "tensor"),
            P("replica", None, "tensor"),
            P("replica", None, "tensor"),
        ),
        check_vma=False,
    )
```

time: 218 us -> 136 us (0.62)
  Pallas kernels: 206 us -> 122 us
  local copies, waits for them, and re-layouts: 11.2 us -> 3.02 us
  other arithmetic: 0 us -> 6.18 us
  between operations: 0.69 us -> 2.87 us
    pallas_call x1, Pallas kernels: 73.9 us -> 3.4 us  [place(): pl.pallas_call(place_kernel, out_shape=(shape, shape), in_specs=[smem, sm...]
    pallas_call x1, Pallas kernels: 126 us -> 115 us  [layer(): pl.pallas_call(functools.partial(layer_kernel, replicas, tensors, tier),...]
    unnamed x22 -> x2, local copies, waits for them, and re-layouts: 8.41 us -> 0.01 us
    select_n x0 -> x5, other arithmetic: none -> 2.9 us  [the longest x1 0.73 us: route(): jnp.where(ahead == half, 0, jnp.where(ahead < half, ahead, ahead - ring))]
    pallas_call x1, Pallas kernels: 6.23 us -> 3.68 us  [plan(): pl.pallas_call(functools.partial(plan_kernel, slots, replicas), out_shape...]
where the time goes in v2:
time: 136 us; the launch traced here: 134 us
  Pallas kernels  122 us (90%)
  other arithmetic  6.18 us (5%)
  local copies, waits for them, and re-layouts  3.02 us (2%)
  between operations  2.87 us (2%)
    pallas_call x1, Pallas kernels, layer(): pl.pallas_call(functools.partial(layer_kernel, replicas, tensors, tier),...  115 us
    pallas_call x1, Pallas kernels, plan(): pl.pallas_call(functools.partial(plan_kernel, slots, replicas), out_shape...  3.68 us
    pallas_call x1, Pallas kernels, place(): pl.pallas_call(place_kernel, out_shape=(shape, shape), in_specs=[smem, sm...  3.4 us

profile of v2, /device:TPU:1, one launch (start us, length us, event | category | flops | bytes accessed | tf_op | source)
XLA Modules:
  0.0 134.1 jit_solution(16623311832880992112)
XLA Ops:
  0.7 0.7 fusion.19
  1.4 0.7 multiply_add_fusion.1
  2.1 0.4 convert_reduce_fusion.2
  2.5 0.5 convert_reduce_fusion.1
  3.0 0.7 add_select_fusion.15
  3.7 0.4 convert_reduce_fusion
  4.1 0.7 fusion.26
  4.8 0.7 select_select_fusion
  5.6 0.7 or_reduce_fusion
  8.2 0.6 select_reduce_fusion.table_ref
  8.8 3.7 %shard_map.130 = (s32[33]{0:T(128)}, s32[224]{0:T(256)S(1)}, f32[128,128]{1,0:T(8,128)S(1)}) custom-call(s32[1]{0:T(128)} %bitcast.me_ref, s32[1024]{0:T(1024)} %len_ref.1, s32[448]{0:T(512)} %src_ref.1, s32[448]{0:T(512)} %dst_ref.1, s32[96]{0:T(128)} %select_reduce_fusion.table_ref), custom_call_target="tpu_custom_call" | custom-call | tf_op jit(solution)/shard_map/pallas_call | solution.py:154
  12.5 2.1 %reshape.84 = bf16[64,5120]{1,0:T(8,128)(2,1)S(1)} reshape(bf16[32,2,5120]{2,1,0:T(2,128)(2,1)} %param.15) | data formatting | bytes 1310720 | tf_op jit(solution)/shard_map/reshape | solution.py:656
  14.6 115.9 %conditional.1 = (bf16[18,512,128]{2,1,0:T(8,128)(2,1)S(1)}, bf16[32,2,640]{2,1,0:T(2,128)(2,1)S(1)}) conditional(s32[]{:T(128)} %clamp.3, (s32[224]{0:T(256)S(1)}, f32[128,128]{1,0:T(8,128)S(1)}, f32[1,128]{1,0:T(1,128)}, bf16[64,5120]{1,0:T(8,128)(2,1)S(1)}, bf16[32,2,512]{2,1,0:T(2,128)(2,1)}, ...), branch_computations={%region_8.9_spmd, %region_9.10_spmd, %region_10.11_spmd, %region_1... | conditional | bytes 163856 | solution.py:665
  14.9 114.7 %branch_2_fun.1 = (bf16[64,640]{1,0:T(8,128)(2,1)}, bf16[18,512,128]{2,1,0:T(8,128)(2,1)S(1)}) custom-call(s32[224]{0:T(256)S(1)} %get-tuple-element.113.scalar_ref, f32[128,128]{1,0:T(8,128)S(1)} %get-tuple-element.114.row_ref, f32[1,128]{1,0:T(1,128)} %get-tuple-element.115.gain_ref, bf16[64,5120]{1,0:T(8,128)(2,1)S(1)} %get-tuple-element.116.hidden_hbm, ...), custom_call_target="tpu_custom_call" | custom-call | tf_op jit(solution)/shard_map/cond/branch_2_fun/pallas_call | solution.py:555
  129.6 0.9 reshape.77
  130.5 0.0 copy-start
  130.5 3.4 %shard_map.131 = (bf16[32,256,128]{2,1,0:T(8,128)(2,1)}, bf16[32,256,128]{2,1,0:T(8,128)(2,1)}) custom-call(s32[224]{0:T(256)S(1)} %get-tuple-element.147.scalar_ref, s32[33]{0:T(128)} %get-tuple-element.150.dead_ref, bf16[18,512,128]{2,1,0:T(8,128)(2,1)S(1)} %get-tuple-element.151.list_hbm), custom_call_target="tpu_custom_call" | custom-call | tf_op jit(solution)/shard_map/pallas_call | solution.py:633
  133.9 0.0 copy-done
  (2 shorter events, 0.0 us)
Async XLA Ops:
  130.5 3.4 %copy-start = (bf16[32,2,640]{2,1,0:T(2,128)(2,1)}, bf16[32,2,640]{2,1,0:T(2,128)(2,1)S(1)}, u32[]{:S(2)}) copy-start(bf16[32,2,640]{2,1,0:T(2,128)(2,1)S(1)} %get-tuple-element.144) | copy-start | bytes 245764

commit v3 on v2

v3 whole, which is shorter than its diff:
```python
import functools
import math

import jax
import jax.numpy as jnp
from jax import lax
from jax.experimental import pallas as pl
from jax.experimental.pallas import tpu as pltpu
from jax.sharding import PartitionSpec as P

EPS = 1e-06
THETA = 1000000.0
MESH = pl.DeviceIdType.MESH
VMEM_LIMIT = 60 * 1024 * 1024
MOVES = 14
STEP_ROWS = 24
TIERS = (((7, 5, 3, 2), 10), ((8, 6, 4, 2), 11), ((9, 7, 5, 3), 12), ((16, 12, 8, 4), 14))
PARTS = 2
Y_WINDOW = 6
HAND_WINDOW = 6
PAUSES = (5, 9, 13, 17, 21)


def route(slots, replicas, me, src, dst, column):
    ring = replicas // 4
    half = ring // 2
    moves = src.shape[1]
    order = lax.broadcasted_iota(jnp.int32, (1, moves), 1)
    exists = order < replicas * MOVES
    from_rep, to_rep = src // slots, dst // slots
    ys, zs, cs = from_rep // (2 * ring), (from_rep // 2) % ring, from_rep % 2
    yd, zd = to_rep // (2 * ring), (to_rep // 2) % ring
    ahead = jnp.where(exists, (zd - zs + ring) % ring, 0)
    group = (yd * ring + zs) * 2 + cs
    distance = jnp.where(ahead <= half, ahead, ring - ahead)
    travels = ahead != 0
    pull = jnp.where((ahead == half) | ~travels, 0, jnp.where(ahead < half, ahead, ahead - ring))
    farthest = ahead == half

    def count(hits):
        return jnp.sum(jnp.where(hits, 1, 0), axis=0, keepdims=True)

    other = column(order)
    before = other < order
    same = column(group) == group
    lean = jnp.sum(jnp.where(same, column(pull), 0), axis=0, keepdims=True)
    rank_far = count((column(jnp.where(farthest, group, -1)) == group) & before)
    way = jnp.where(ahead < half, 0, 1)
    for i in range(4):
        back = lean > 0
        way = jnp.where(farthest & (rank_far == i), jnp.where(back, 1, 0), way)
        lean = lean + jnp.where(back, -half, half)
    list_key = group * 2 + way
    sort_key = (list_key * 8 + 7 - distance) * moves + order
    other_list = column(jnp.where(travels, list_key, -1))
    place_in = count((other_list == list_key) & (column(sort_key) < sort_key))
    spot = 2 * place_in + way
    crosses = travels & (ys != yd)
    y_key = from_rep * 64 + spot
    other_y = column(jnp.where(crosses, y_key, -1))
    y_rank = count((other_y >= from_rep * 64) & (other_y < y_key))

    tier = jnp.full((1, 1), len(TIERS) - 1, jnp.int32)
    for i, (caps, y_cap) in reversed(list(enumerate(TIERS[:-1]))):
        reach = sum(jnp.where(place_in < c, 1, 0) for c in caps)
        misfit = travels & ((distance > reach) | (crosses & (y_rank >= y_cap)))
        tier = jnp.where(jnp.sum(jnp.where(misfit, 1, 0), axis=1, keepdims=True) == 0, i, tier)

    my_y, my_z, my_c = me // (2 * ring), (me // 2) % ring, me % 2
    mine = exists & (from_rep == me)
    in_group = travels & (group == (my_y * ring + my_z) * 2 + my_c)
    kind = jnp.where(ys == yd, 0, jnp.where(cs == to_rep % 2, 1, 2))
    address = jnp.where(
        in_group,
        spot,
        jnp.where(
            mine,
            jnp.where(travels, 32 + y_rank, 48 + kind),
            jnp.where(exists & (to_rep == me), 64 + dst % slots, -1),
        ),
    )
    code = (((place_in * 2 + way) * 8 + distance) * 4 + kind) * 1024 + src + 1
    value = jnp.where(in_group, jnp.where(mine, src % slots, slots + y_rank), jnp.where(mine, src % slots, code))
    width = 128
    lane = lax.broadcasted_iota(jnp.int32, (1, width), 1)
    hit = column(address)[:, :width] == lane
    table = jnp.sum(jnp.where(hit, column(value)[:, :width], 0), axis=0, keepdims=True)
    return jnp.where(lane == width - 1, tier, table)


INJECT, ACROSS, NEAR, LIVE, LENGTH, LANE, SPOT, KIND, TABLE = 0, 32, 48, 64, 96, 128, 144, 160, 176


def plan_kernel(
    slots,
    replicas,
    me_ref,
    len_ref,
    src_ref,
    src_row,
    dst_row,
    tier_ref,
    dead_ref,
    out_ref,
    row_ref,
    mark,
    padded,
    table_vmem,
    table_ref,
    sem,
):
    me = me_ref[0]
    moves = padded.shape[1]
    count = src_row.shape[1]
    padded[...] = jnp.zeros_like(padded)
    padded[0:1, :count] = src_row[...]
    padded[1:2, :count] = dst_row[...]

    def column(row):
        tall = jnp.broadcast_to(row.astype(jnp.float32), (128, moves))
        tall = jnp.concatenate([tall[:, i : i + 128].T for i in range(0, moves, 128)], axis=0).astype(jnp.int32)
        return jnp.concatenate([tall] * (moves // 128), axis=1)

    table_vmem[...] = route(slots, replicas, me, padded[0:1, :], padded[1:2, :], column)
    fetch = pltpu.make_async_copy(table_vmem, table_ref, sem)
    fetch.start()

    def clear(i, _):
        mark[i] = 0
        return 0

    lax.fori_loop(0, slots, clear, 0, unroll=8)

    def out(k, _):
        mark[src_ref[me * MOVES + k] % slots] = 1
        return 0

    lax.fori_loop(0, MOVES, out, 0, unroll=2)
    fetch.wait()
    tier_ref[0] = table_ref[0, 127]

    def copy(i, _):
        out_ref[INJECT + i] = table_ref[0, i]
        return 0

    lax.fori_loop(0, 64, copy, 0, unroll=8)

    def each(s, counts):
        kept_count, in_count, dead_count = counts
        code = table_ref[0, 64 + s]
        incoming = code > 0
        source = jnp.where(incoming, (code - 1) % 1024, me * slots + s)
        length = len_ref[source]
        stays = jnp.logical_not(incoming) & (mark[s] == 0) & (length > 0)
        alive = incoming | stays
        length = jnp.where(alive, length, 0)
        at = jnp.where(incoming, slots - 2 * MOVES + in_count, kept_count)
        where = jnp.where(alive, at, slots - 1)
        out_ref[LIVE + where] = s
        out_ref[LENGTH + where] = length
        dead_ref[dead_count] = s
        rest = (code - 1) // 1024
        kind = rest % 4
        distance = (rest // 4) % 8
        way = (rest // 32) % 2
        source_rep = source // slots
        slot_in = jnp.where(incoming, in_count, MOVES)
        other_core = jnp.where(source_rep % 2 == me % 2, 0, 1)
        out_ref[LANE + slot_in] = (other_core * 2 + way) * 4 + distance - 1
        out_ref[SPOT + slot_in] = rest // 64
        out_ref[KIND + slot_in] = jnp.where(distance == 0, kind, -1)
        for t in range(2):
            row_ref[pl.ds(2 * s + t, 1), :] = jnp.full((1, 128), length + t, jnp.int32).astype(jnp.float32)
            row_ref[pl.ds(2 * (slots + s) + t, 1), :] = jnp.full(
                (1, 128), jnp.where(alive, at + t * STEP_ROWS, -1), jnp.int32
            ).astype(jnp.float32)
        one = jnp.int32(1)
        return (
            kept_count + jnp.where(stays, one, 0),
            in_count + jnp.where(incoming, one, 0),
            dead_count + jnp.where(alive, 0, one),
        )

    zero = jnp.int32(0)
    lax.fori_loop(0, slots, each, (zero, zero, zero), unroll=2)


def plan(me, lengths, move_src, move_dst, slots, replicas):
    smem = pl.BlockSpec(memory_space=pltpu.SMEM)
    vmem = pl.BlockSpec(memory_space=pltpu.VMEM)
    ints = lambda n: jax.ShapeDtypeStruct((n,), jnp.int32)
    moves = -(-move_src.shape[0] // 128) * 128
    return pl.pallas_call(
        functools.partial(plan_kernel, slots, replicas),
        out_shape=(ints(1), ints(slots + 1), ints(TABLE), jax.ShapeDtypeStruct((4 * slots, 128), jnp.float32)),
        in_specs=[smem] * 3 + [vmem] * 2,
        out_specs=(smem,) * 3 + (vmem,),
        scratch_shapes=[
            pltpu.SMEM((slots,), jnp.int32),
            pltpu.VMEM((8, moves), jnp.int32),
            pltpu.VMEM((1, 128), jnp.int32),
            pltpu.SMEM((1, 128), jnp.int32),
            pltpu.SemaphoreType.DMA,
        ],
    )(me, lengths, move_src, move_src.reshape(1, -1), move_dst.reshape(1, -1))


def crossings(y_cap):
    return [(b, part) for low in range(0, y_cap, 2) for part in range(PARTS) for b in range(low, min(low + 2, y_cap))]


def timetable(caps, y_cap):
    step, lag = 1.0 / PARTS, 0.5
    across = {key: (n + 1) * step + lag for n, key in enumerate(crossings(y_cap))}
    ready = [
        (across[min(i, y_cap - 1), part] + 0.01 * max(0, i - y_cap), 1, "inject", i % 2, 1, i // 2, part)
        for i in range(2 * caps[0])
        for part in range(PARTS)
    ]
    free = [0.0, 0.0]
    events = []
    while ready:
        ready.sort()
        time, _, what, way, hop, spot, part = event = ready.pop(0)
        events.append(event[2:])
        if what == "inject" or (hop < len(caps) and spot < caps[hop]):
            free[way] = max(free[way], time) + step
            onward = hop if what == "inject" else hop + 1
            ready.append((free[way] + lag, 0, "pass", way, onward, spot, part))
    return events


class Ring:
    def __init__(self, tier, replicas, me, scalars, caches, arrived, inject, across, across_in, near, *sems):
        self.caps, self.y_cap = tier
        self.me, self.scalars, self.caches = me, scalars, caches
        self.arrived, self.inject, self.across, self.across_in, self.near = arrived, inject, across, across_in, near
        self.hop_send, self.hop_recv, self.core_send, self.core_recv, self.y_send, self.y_recv, self.near_send, self.near_recv = sems
        half = replicas // 2
        line = (me // half) * half
        ahead = line + lax.rem(me - line + 2, half)
        behind = line + lax.rem(me - line + half - 2, half)
        core = me + 1 - 2 * lax.rem(me, 2)
        opposite = lax.rem(me + half, replicas)
        both = lax.rem(core + half, replicas)
        self.ways = (ahead, behind)
        self.core, self.opposite = core, opposite
        self.near_peers = (core, opposite, both)
        self.partners = 5
        self.events = timetable(self.caps, self.y_cap)
        self.lanes = 2 * sum(self.caps)

    def greet(self, barrier):
        for peer in self.ways + self.near_peers:
            pl.semaphore_signal(barrier, inc=1, device_id={"replica": peer}, device_id_type=MESH)

    def copy(self, source, target, send_sem, recv_sem, peer):
        return pltpu.make_async_remote_copy(
            src_ref=source, dst_ref=target, send_sem=send_sem, recv_sem=recv_sem, device_id={"replica": peer}, device_id_type=MESH
        )

    def lane(self, way, hop, spot):
        return way * sum(self.caps) + sum(self.caps[: hop - 1]) + spot

    def half(self, ref, at, part):
        rows = self.caches[0].shape[1]
        return ref.at[at, pl.ds(part * rows, rows)]

    def cross(self, b, part):
        at = b * PARTS + part
        return self.copy(
            self.half(self.across, b, part), self.half(self.across_in, b, part), self.y_send.at[at], self.y_recv.at[at], self.opposite
        )

    def next_door(self, j):
        target = self.arrived.at[2 * self.lanes + j]
        return self.copy(self.near.at[j], target, self.near_send.at[j], self.near_recv.at[j], self.near_peers[j])

    def hop(self, way, hop, spot, part):
        source = (self.inject, 2 * spot + way) if hop == 1 else (self.arrived, self.lane(way, hop - 1, spot))
        to = self.lane(way, hop, spot)
        at = to * PARTS + part
        return self.copy(
            self.half(*source, part), self.half(self.arrived, to, part), self.hop_send.at[at], self.hop_recv.at[at], self.ways[way]
        )

    def hand_over(self, way, hop, spot, part):
        lane = self.lane(way, hop, spot)
        at = lane * PARTS + part
        return self.copy(
            self.half(self.arrived, lane, part),
            self.half(self.arrived, self.lanes + lane, part),
            self.core_send.at[at],
            self.core_recv.at[at],
            self.core,
        )

    def pack(self, target, at, slot, parts):
        rows = self.caches[0].shape[1]
        for part in parts:
            target[at, part * rows : (part + 1) * rows, :] = self.caches[part][slot]

    def begin(self, n):
        order = crossings(self.y_cap)
        if n < len(order):
            b, part = order[n]
            self.pack(self.across, b, self.scalars[ACROSS + b], (part,))
            self.cross(b, part).start()
        elif n < len(order) + 3:
            j = n - len(order)
            self.pack(self.near, j, self.scalars[NEAR + j], range(PARTS))
            self.next_door(j).start()

    def enter(self, way, spot, part, crossed):
        slots, rows, _ = self.caches[0].shape
        i = 2 * spot + way
        here = slice(part * rows, (part + 1) * rows)
        code = self.scalars[INJECT + i]
        block = self.caches[part][jnp.where(code < slots, code, 0)]
        if crossed == len(crossings(self.y_cap)):
            other = self.across_in[jnp.where(code < slots, 0, code - slots), here, :]
            block = jnp.where(code < slots, block, other)
        else:
            for b in range(min(i + 1, self.y_cap)):
                block = jnp.where(code == slots + b, self.across_in[b, here, :], block)
        self.inject[i, here, :] = block
        self.hop(way, 1, spot, part).start()

    def carry(self, pauses):
        order = crossings(self.y_cap)
        for n in range(Y_WINDOW):
            self.begin(n)
        crossed = 0
        pauses = dict(pauses)
        over = []
        for count, (what, way, hop, spot, part) in enumerate(self.events):
            if what == "inject":
                needed = order.index((min(2 * spot + way, self.y_cap - 1), part)) + 1
                while crossed < needed:
                    self.cross(*order[crossed]).wait_recv()
                    self.begin(crossed + Y_WINDOW)
                    crossed += 1
                self.enter(way, spot, part, crossed)
            else:
                self.hop(way, hop, spot, part).wait_recv()
                if hop < len(self.caps) and spot < self.caps[hop]:
                    self.hop(way, hop + 1, spot, part).start()
                self.hand_over(way, hop, spot, part).start()
                over.append((way, hop, spot, part))
                if len(over) > HAND_WINDOW:
                    self.hand_over(*over[-1 - HAND_WINDOW]).wait()
            if count in pauses:
                pauses.pop(count)()
        for pause in pauses.values():
            pause()
        for n in range(crossed, len(order)):
            self.cross(*order[n]).wait_recv()
        for n in range(max(Y_WINDOW, crossed + Y_WINDOW), len(order) + 3):
            self.begin(n)
        for j in range(3):
            self.next_door(j).wait_recv()
        for key in over[-HAND_WINDOW:]:
            self.hand_over(*key).wait()

    def where(self, i):
        kind, lane = self.scalars[KIND + i], self.scalars[LANE + i]
        first = 0
        for n in range(2 * 2 * len(self.caps)):
            way, hop = n // len(self.caps) % 2, n % len(self.caps) + 1
            first = jnp.where(lane == n, n // (2 * len(self.caps)) * self.lanes + self.lane(way, hop, 0), first)
        return jnp.where(kind >= 0, 2 * self.lanes + kind, first + self.scalars[SPOT + i])

    def finish(self):
        for b, part in crossings(self.y_cap):
            self.cross(b, part).wait_send()
        for j in range(3):
            self.next_door(j).wait_send()
        for what, way, hop, spot, part in self.events:
            if what == "pass":
                self.hop(way, hop, spot, part).wait_send()


def layer_kernel(
    replicas,
    tensors,
    tier,
    scalar_ref,
    row_ref,
    gain_ref,
    hidden_hbm,
    query_hbm,
    ck_hbm,
    cv_hbm,
    kw_hbm,
    vw_hbm,
    ow_hbm,
    branch_ref,
    list_hbm,
    ck,
    cv,
    hid,
    qry,
    kw,
    vw,
    ow,
    flat,
    listed,
    fresh_k,
    fresh_v,
    mix,
    score,
    rs_stage,
    rs_recv,
    reduced,
    in_sem,
    rs_send_sem,
    rs_recv_sem,
    list_sem,
    *transport,
):
    me = lax.axis_index("replica")
    at = lax.axis_index("tensor")
    slots, rows, width = ck.shape
    live = listed.shape[0]
    kept = live - MOVES
    groups = query_hbm.shape[2] // width

    loads = [
        pltpu.make_async_copy(source, target, in_sem.at[i])
        for i, (source, target) in enumerate(
            (
                (ck_hbm, ck),
                (cv_hbm, cv),
                (hidden_hbm, hid),
                (kw_hbm, kw),
                (vw_hbm, vw),
                (query_hbm, qry),
                (ow_hbm, ow),
            )
        )
    ]
    loads[0].start()
    loads[1].start()

    caches = (ck, cv)
    road = Ring(tier, replicas, me, scalar_ref, caches, *transport)

    barrier = pltpu.get_barrier_semaphore()
    road.greet(barrier)

    def greet_tensor(j, _):
        pl.semaphore_signal(barrier, inc=1, device_id={"tensor": lax.rem(at + j, tensors)}, device_id_type=MESH)
        return 0

    lax.fori_loop(1, tensors, greet_tensor, 0)
    pl.semaphore_wait(barrier, road.partners + tensors - 1)

    loads[0].wait()
    loads[1].wait()
    for load in loads[2:]:
        load.start()

    def flatten():
        loads[2].wait()
        for s in range(slots):
            flat[2 * s : 2 * s + 2, :] = hid[s]

    def project_keys():
        loads[3].wait()
        fresh_k[...] = jnp.dot(flat[...], kw[...], preferred_element_type=jnp.float32)

    def project_values():
        loads[4].wait()
        raw_v = jnp.dot(flat[...], vw[...], preferred_element_type=jnp.float32)
        fresh_v[...] = raw_v.astype(jnp.bfloat16).astype(jnp.float32)

    lane = lax.broadcasted_iota(jnp.int32, (1, width), 1)

    def rotate_keys():
        raw_k = fresh_k[...]
        mean_square = jnp.mean(raw_k * raw_k, axis=-1, keepdims=True)
        normed = raw_k * lax.rsqrt(mean_square + EPS) * gain_ref[...]
        half = width // 2
        index = jnp.where(lane < half, lane, lane - half).astype(jnp.float32)
        angles = row_ref[: 2 * slots, :] * jnp.exp(index * (-2.0 * math.log(THETA) / width))
        turned = pltpu.roll(normed, half, 1)
        sine = jnp.sin(angles)
        rotated = normed * jnp.cos(angles) + turned * jnp.where(lane < half, -sine, sine)
        fresh_k[...] = rotated.astype(jnp.bfloat16).astype(jnp.float32)

    row_ids = lax.broadcasted_iota(jnp.int32, (rows, width), 0)
    column_ids = lax.broadcasted_iota(jnp.int32, (2 * groups, rows), 1)
    step_ids = lax.broadcasted_iota(jnp.int32, (2 * groups, rows), 0) % 2

    def placed(stored, fresh, slot, length):
        full = jnp.where(row_ids < length, stored.astype(jnp.float32), 0.0)
        full = jnp.where(row_ids == length, fresh[pl.ds(2 * slot, 1), :], full)
        full = jnp.where(row_ids == length + 1, fresh[pl.ds(2 * slot + 1, 1), :], full)
        return full.astype(jnp.bfloat16)

    heads = 2 * groups

    def attend(first, count, stored, unroll):
        def fill(i, _):
            e = first + i
            slot, length = scalar_ref[LIVE + e], scalar_ref[LENGTH + e]
            stored_k, stored_v = stored(i)
            listed[e, :rows, :] = placed(stored_k, fresh_k, slot, length)
            listed[e, rows:, :] = placed(stored_v, fresh_v, slot, length)
            pltpu.make_async_copy(listed.at[e], list_hbm.at[e], list_sem.at[e]).start()
            return 0

        def weigh(i, _):
            e = first + i
            slot, length = scalar_ref[LIVE + e], scalar_ref[LENGTH + e]
            q = qry[slot].astype(jnp.float32)
            q = jnp.concatenate([q[:, g * width : (g + 1) * width] for g in range(groups)], axis=0).astype(jnp.bfloat16)
            scores = lax.dot_general(
                q, listed[e, :rows, :], (((1,), (1,)), ((), ())), preferred_element_type=jnp.float32
            ) * width ** (-0.5)
            at = pl.ds(pl.multiple_of(e * heads, heads), heads)
            score[at, :] = jnp.where(column_ids <= length + step_ids, scores, -jnp.inf)
            return 0

        def blend(i, _):
            e = first + i
            at = pl.ds(pl.multiple_of(e * heads, heads), heads)
            mix[at, :] = jnp.dot(score[at, :].astype(jnp.bfloat16), listed[e, rows:, :], preferred_element_type=jnp.float32)
            return 0

        lax.fori_loop(0, count, fill, 0, unroll=2)
        lax.fori_loop(0, count, weigh, 0, unroll=unroll)
        every = slice(first * heads, (first + count) * heads)
        scores = score[every, :]
        weights = jnp.exp(scores - jnp.max(scores, axis=-1, keepdims=True))
        score[every, :] = weights / jnp.sum(weights, axis=-1, keepdims=True)
        lax.fori_loop(0, count, blend, 0, unroll=unroll)

    def own(i):
        slot = scalar_ref[LIVE + i]
        return ck[slot], cv[slot]

    def brought(i):
        source = road.where(i)
        return road.arrived[source, :rows, :], road.arrived[source, rows:, :]

    def attend_kept():
        loads[5].wait()
        attend(0, kept, own, kept)
        mix[heads * live :, :] = jnp.zeros((mix.shape[0] - heads * live, width), jnp.float32)
        reduced[...] = jnp.zeros_like(reduced)
        loads[6].wait()

    road.carry(zip(PAUSES, (flatten, project_keys, project_values, rotate_keys, attend_kept)))
    attend(kept, MOVES, brought, 7)

    steps = [
        jnp.concatenate([mix[pl.ds(2 * g + t, STEP_ROWS, stride=heads), :] for g in range(groups)], axis=1)
        for t in range(2)
    ]
    mixture = jnp.concatenate(steps, axis=0).astype(jnp.bfloat16)
    out_width = branch_ref.shape[1]

    def part(j):
        first = pl.multiple_of(lax.rem(at + j, tensors) * out_width, 128)
        return jnp.dot(mixture, ow[:, pl.ds(first, out_width)], preferred_element_type=jnp.float32)

    def give(j):
        return pltpu.make_async_remote_copy(
            src_ref=rs_stage.at[j],
            dst_ref=rs_recv.at[j],
            send_sem=rs_send_sem.at[j],
            recv_sem=rs_recv_sem.at[j],
            device_id={"tensor": lax.rem(at + j, tensors)},
            device_id_type=MESH,
        )

    def give_part(j, _):
        rs_stage[j] = part(j).astype(jnp.bfloat16)
        give(j).start()
        return 0

    lax.fori_loop(1, tensors, give_part, 0)
    total = part(0)
    road.finish()
    for j in range(1, tensors):
        give(j).wait_recv()
        total = total + rs_recv[j].astype(jnp.float32)
    reduced[: 2 * STEP_ROWS, :] = total.astype(jnp.bfloat16)
    rows_at = row_ref[2 * slots :, :]
    pick = (lane.astype(jnp.float32) == rows_at).astype(jnp.float32).astype(jnp.bfloat16)
    branch_ref[...] = jnp.dot(pick, reduced[...], preferred_element_type=jnp.float32).astype(jnp.bfloat16)

    def given(j, _):
        give(j).wait_send()
        return 0

    lax.fori_loop(1, tensors, given, 0)

    def written(e, _):
        pltpu.make_async_copy(listed.at[e], list_hbm.at[e], list_sem.at[e]).wait()
        return 0

    lax.fori_loop(0, live, written, 0)


def layer(tier, replicas, tensors, scalars, rows_at, gain, *operands):
    hidden, queries, cache_keys, cache_values, key_weight, value_weight, out_weight = operands
    slots, rows, width = cache_keys.shape
    live = slots - MOVES
    groups = queries.shape[2] // width
    out_width = out_weight.shape[1] // tensors
    smem = pl.BlockSpec(memory_space=pltpu.SMEM)
    vmem = pl.BlockSpec(memory_space=pltpu.VMEM)
    any_ = pl.BlockSpec(memory_space=pl.ANY)
    bf16 = jnp.bfloat16
    dma = pltpu.SemaphoreType.DMA

    def rollouts(n):
        return pltpu.VMEM((n, 2 * rows, width), bf16)

    caps, y_cap = tier
    lanes = 2 * sum(caps)
    transport = [
        rollouts(2 * lanes + 3),
        rollouts(2 * caps[0]),
        rollouts(y_cap),
        rollouts(y_cap),
        rollouts(3),
    ]
    sizes = (lanes * PARTS, lanes * PARTS, lanes * PARTS, lanes * PARTS, y_cap * PARTS, y_cap * PARTS, 3, 3)
    transport += [dma((n,)) for n in sizes]
    return pl.pallas_call(
        functools.partial(layer_kernel, replicas, tensors, tier),
        out_shape=(
            jax.ShapeDtypeStruct((2 * slots, out_width), bf16),
            jax.ShapeDtypeStruct((live, 2 * rows, width), bf16),
        ),
        in_specs=[smem] + [vmem] * 2 + [any_] * len(operands),
        out_specs=(vmem, any_),
        scratch_shapes=[
            pltpu.VMEM(cache_keys.shape, bf16),
            pltpu.VMEM(cache_values.shape, bf16),
            pltpu.VMEM(hidden.shape, bf16),
            pltpu.VMEM(queries.shape, bf16),
            pltpu.VMEM(key_weight.shape, bf16),
            pltpu.VMEM(value_weight.shape, bf16),
            pltpu.VMEM(out_weight.shape, bf16),
            pltpu.VMEM((2 * slots, hidden.shape[2]), bf16),
            pltpu.VMEM((live, 2 * rows, width), bf16),
            pltpu.VMEM((2 * slots, width), jnp.float32),
            pltpu.VMEM((2 * slots, width), jnp.float32),
            pltpu.VMEM((2 * groups * STEP_ROWS, width), jnp.float32),
            pltpu.VMEM((2 * groups * live, rows), jnp.float32),
            pltpu.VMEM((tensors, 2 * STEP_ROWS, out_width), bf16),
            pltpu.VMEM((tensors, 2 * STEP_ROWS, out_width), bf16),
            pltpu.VMEM((128, out_width), bf16),
            dma((len(operands),)),
            dma((tensors,)),
            dma((tensors,)),
            dma((live,)),
        ]
        + transport,
        compiler_params=pltpu.CompilerParams(
            collective_id=TIERS.index(tier),
            has_side_effects=True,
            vmem_limit_bytes=VMEM_LIMIT,
        ),
    )(scalars, rows_at, gain, *operands)


def place_kernel(scalar_ref, dead_ref, flat_ref, list_hbm, branch_ref, keys_hbm, values_hbm, listed, zeros, sem):
    rows = zeros.shape[0]
    live = listed.shape[0]
    load = pltpu.make_async_copy(list_hbm, listed, sem.at[live + MOVES, 0])
    load.start()
    zeros[...] = jnp.zeros_like(zeros)

    def copies(e):
        slot = scalar_ref[LIVE + e]
        return (
            pltpu.make_async_copy(listed.at[e, pl.ds(0, rows)], keys_hbm.at[slot], sem.at[e, 0]),
            pltpu.make_async_copy(listed.at[e, pl.ds(rows, rows)], values_hbm.at[slot], sem.at[e, 1]),
        )

    def clears(e):
        slot = dead_ref[e]
        return (
            pltpu.make_async_copy(zeros, keys_hbm.at[slot], sem.at[live + e, 0]),
            pltpu.make_async_copy(zeros, values_hbm.at[slot], sem.at[live + e, 1]),
        )

    def run(make, count, act):
        def each(e, _):
            for copy in make(e):
                getattr(copy, act)()
            return 0

        lax.fori_loop(0, count, each, 0)

    run(clears, MOVES, "start")
    load.wait()
    run(copies, live, "start")
    for s in range(branch_ref.shape[0]):
        branch_ref[s] = flat_ref[2 * s : 2 * s + 2, :]
    run(clears, MOVES, "wait")
    run(copies, live, "wait")


def place(scalars, dead_slots, branch, listed, slots):
    live, both, width = listed.shape
    shape = jax.ShapeDtypeStruct((slots, both // 2, width), listed.dtype)
    smem = pl.BlockSpec(memory_space=pltpu.SMEM)
    vmem = pl.BlockSpec(memory_space=pltpu.VMEM)
    any_ = pl.BlockSpec(memory_space=pl.ANY)
    return pl.pallas_call(
        place_kernel,
        out_shape=(jax.ShapeDtypeStruct((slots, 2, branch.shape[1]), branch.dtype), shape, shape),
        in_specs=[smem, smem, vmem, any_],
        out_specs=(vmem, any_, any_),
        scratch_shapes=[
            pltpu.VMEM(listed.shape, listed.dtype),
            pltpu.VMEM((both // 2, width), listed.dtype),
            pltpu.SemaphoreType.DMA((slots + 1, 2)),
        ],
    )(scalars, dead_slots, branch, listed)


def shards(hidden, queries, cache_keys, cache_values, key_weight, value_weight, key_gain, out_weight, lengths, move_src, move_dst):
    slots = cache_keys.shape[0]
    replicas, tensors = lax.axis_size("replica"), lax.axis_size("tensor")
    me = lax.axis_index("replica").astype(jnp.int32)
    tier, dead, scalars, rows_at = plan(me.reshape(1), lengths, move_src, move_dst, slots, replicas)
    operands = (
        scalars,
        rows_at,
        key_gain.reshape(1, -1),
        hidden,
        queries,
        cache_keys,
        cache_values,
        key_weight,
        value_weight,
        out_weight,
    )
    branches = [functools.partial(layer, t, replicas, tensors) for t in TIERS]
    branch, listed = lax.switch(tier[0], branches, *operands)
    return place(scalars, dead, branch, listed, slots)


def solution(mesh):
    placed = (
        P("replica", None, None),
        P("replica", None, "tensor"),
        P("replica", None, "tensor"),
        P("replica", None, "tensor"),
        P(None, "tensor"),
        P(None, "tensor"),
        P(),
        P("tensor", None),
        P(),
        P(),
        P(),
    )
    return jax.shard_map(
        shards,
        mesh=mesh,
        in_specs=placed,
        out_specs=(
            P("replica", None, "tensor"),
            P("replica", None, "tensor"),
            P("replica", None, "tensor"),
        ),
        check_vma=False,
    )
```

time: 136 us -> 107 us (0.79)
  Pallas kernels: 122 us -> 104 us
  other arithmetic: 6.18 us -> 0 us
  local copies, waits for them, and re-layouts: 3.02 us -> 0 us
    pallas_call x1, Pallas kernels: 115 us -> 95.1 us  [layer(): pl.pallas_call(functools.partial(layer_kernel, replicas, tensors, tier),...]
    reshape x2 -> x0, local copies, waits for them, and re-layouts: 3.02 us -> none  [the longest x1 2.09 us: shards(): hidden.reshape(2 * slots, -1)]
    select_n x5 -> x0, other arithmetic: 2.9 us -> none  [the longest x1 0.73 us: route(): jnp.where(ahead == half, 0, jnp.where(ahead < half, ahead, ahead - ring))]
    reduce_sum x4 -> x0, other arithmetic: 1.89 us -> none  [the longest x1 0.63 us: route(): jnp.sum(jnp.where(wanted[:, None] == address[None, :], value[None, :], 0)...]
where the time goes in v3:
time: 107 us; the launch traced here: 106 us
  Pallas kernels  104 us (97%)
  between operations  1.52 us (1%)
    pallas_call x1, Pallas kernels, layer(): pl.pallas_call(functools.partial(layer_kernel, replicas, tensors, tier),...  95.1 us
    pallas_call x1, Pallas kernels, plan(): pl.pallas_call(functools.partial(plan_kernel, slots, replicas), out_shape...  4.96 us
    pallas_call x1, Pallas kernels, place(): pl.pallas_call(place_kernel, out_shape=(jax.ShapeDtypeStruct((slots, 2, b...  4.03 us

profile of v3, /device:TPU:1, one launch (start us, length us, event | category | flops | bytes accessed | tf_op | source)
XLA Modules:
  0.0 106.3 jit_solution(7113184425734770732)
XLA Ops:
  0.6 5.0 %shard_map.130 = (s32[1]{0:T(128)}, s32[33]{0:T(128)}, s32[176]{0:T(256)S(1)}, f32[128,128]{1,0:T(8,128)S(1)}) custom-call(s32[1]{0:T(128)} %bitcast.me_ref, s32[1024]{0:T(1024)} %len_ref.1, s32[448]{0:T(512)} %src_ref.1, s32[1,448]{1,0:T(1,128)} %bitcast.5, s32[1,448]{1,0:T(1,128)} %bitcast.10), custom_call_target="tpu_custom_call" | custom-call | tf_op jit(solution)/shard_map/pallas_call | solution.py:193
  6.3 95.8 %conditional.1 = ((bf16[64,640]{1,0:T(8,128)(2,1)S(1)}, bf16[18,512,128]{2,1,0:T(8,128)(2,1)S(1)})) conditional(s32[]{:T(128)} %bitcast.3, (s32[176]{0:T(256)S(1)}, f32[128,128]{1,0:T(8,128)S(1)}, f32[1,128]{1,0:T(1,128)}, bf16[32,2,5120]{2,1,0:T(2,128)(2,1)}, bf16[32,2,512]{2,1,0:T(2,128)(2,1)}, ...), branch_computations={%region_0.0_spmd, %region_1.0_spmd, %region_2.0_spmd, %region_3.0_... | conditional | bytes 8 | solution.py:747
  6.5 95.1 %branch_1_fun.1 = (bf16[64,640]{1,0:T(8,128)(2,1)S(1)}, bf16[18,512,128]{2,1,0:T(8,128)(2,1)S(1)}) custom-call(s32[176]{0:T(256)S(1)} %get-tuple-element.90.scalar_ref, f32[128,128]{1,0:T(8,128)S(1)} %get-tuple-element.91.row_ref, f32[1,128]{1,0:T(1,128)} %get-tuple-element.92.gain_ref, bf16[32,2,5120]{2,1,0:T(2,128)(2,1)} %get-tuple-element.93.hidden_hbm, ...), custom_call_target="tpu_custom_call" | custom-call | tf_op jit(solution)/shard_map/cond/branch_1_fun/pallas_call | solution.py:633
  102.1 4.0 %shard_map.131 = (bf16[32,2,640]{2,1,0:T(2,128)(2,1)}, bf16[32,256,128]{2,1,0:T(8,128)(2,1)}, bf16[32,256,128]{2,1,0:T(8,128)(2,1)}) custom-call(s32[176]{0:T(256)S(1)} %get-tuple-element.129.scalar_ref, s32[33]{0:T(128)} %get-tuple-element.130.dead_ref, bf16[64,640]{1,0:T(8,128)(2,1)S(1)} %get-tuple-element.133.flat_ref, ...), custom_call_target="tpu_custom_call" | custom-call | tf_op jit(solution)/shard_map/pallas_call | solution.py:716
